TPU v7x, 32 devices: a whole 2x2x4 slice. The times are simulated.
32 devices in a mesh: ctx: 8 (over z, x), fsdp: 4 (over y, core).
Axes of the slice: x: 2, y: 2, z: 4, core: 2. Of those that a mesh axis runs over, the one named last changes fastest.
Arguments:
- tokens: bfloat16 [2, 4, 2048, 1024], P(None, 'fsdp', 'ctx'), may hold values from -6 to 6
- lengths: int32 [2, 4], P(None, 'fsdp'), may hold values from 512 to 2048, as said below
- w_query: bfloat16 [1024, 1024], P('fsdp'), may hold values from -0.1875 to 0.1875
- w_key: bfloat16 [1024, 1024], P('fsdp'), may hold values from -0.1875 to 0.1875
- w_value: bfloat16 [1024, 1024], P('fsdp'), may hold values from -0.1875 to 0.1875
- w_mixgate: bfloat16 [1024, 1024], P('fsdp'), may hold values from -0.1875 to 0.1875
- w_output: bfloat16 [1024, 1024], P('fsdp'), may hold values from -1.5 to 1.5
- w_ffgate: bfloat16 [1024, 2816], P('fsdp'), may hold values from -0.1875 to 0.1875
- w_ffup: bfloat16 [1024, 2816], P('fsdp'), may hold values from -0.1875 to 0.1875
- w_ffdown: bfloat16 [2816, 1024], P('fsdp'), may hold values from -0.21875 to 0.21875
- conv_weight: float32 [3, 4, 1024], replicated, may hold values from -3 to 3
- norm_first: float32 [1024], replicated, may hold values from 0.5 to 1.5
- norm_second: float32 [1024], replicated, may hold values from 0.5 to 1.5
- ridge_log: float32 [1024], replicated, may hold values from 0 to 2.3
- out_grad: bfloat16 [2, 4, 2048, 1024], P(None, 'fsdp', 'ctx'), may hold values from -6 to 6
Outputs:
- result: bfloat16 [2, 4, 2048, 1024], P(None, 'fsdp', 'ctx')
- input_grad: bfloat16 [2, 4, 2048, 1024], P(None, 'fsdp', 'ctx')
- query_grad: float32 [1024, 1024], P(None, ('ctx', 'fsdp'))
- key_grad: float32 [1024, 1024], P(None, ('ctx', 'fsdp'))
- value_grad: float32 [1024, 1024], P(None, ('ctx', 'fsdp'))
- mixgate_grad: float32 [1024, 1024], P(None, ('ctx', 'fsdp'))
- output_grad: float32 [1024, 1024], P(None, ('ctx', 'fsdp'))
- ffgate_grad: float32 [1024, 2816], P(None, ('ctx', 'fsdp'))
- ffup_grad: float32 [1024, 2816], P(None, ('ctx', 'fsdp'))
- ffdown_grad: float32 [2816, 1024], P(None, ('ctx', 'fsdp'))
- conv_grad: float32 [3, 4, 1024], P(None, None, ('ctx', 'fsdp'))
- first_gain_grad: float32 [1024], P(('ctx', 'fsdp'))
- second_gain_grad: float32 [1024], P(('ctx', 'fsdp'))
- ridge_grad: float32 [1024], P(('ctx', 'fsdp'))
Inputs may be any that keep to these rules, and one draw needn't show every extreme that they name: `lengths`: in each micro-batch one sequence, drawn from the seed, has length exactly 2048.
All inputs are finite; a program needn't handle non-finite values.
Results may differ from a plain program's by a relative error of at most 0.025.
Values may be sent and summed in bfloat16 or wider, within the bound.
No kernel may reach another device: no remote copies, remote signals or barrier semaphores. Data moves between devices by JAX's collectives and lax.ppermute only.
A program may use at most 448 MiB of HBM per device.

v0:
```python
from functools import partial

import jax
import jax.numpy as jnp
from jax import lax
from jax.sharding import PartitionSpec as P

HEAD_COUNT = 8
HEAD_SIZE = 128
C = 128
ITERS = 2


EPS = 1e-06
HIGH = lax.Precision.HIGHEST


def extended_2(value, sides, width):
    for axis, dim in sides:
        count, length = (lax.axis_size(axis), value.shape[dim])
        up = [(i, (i + 1) % count) for i in range(count - 1)]
        down = [(j, i) for i, j in up]
        last = lax.slice_in_dim(value, length - width, length, axis=dim)
        first = lax.slice_in_dim(value, 0, width, axis=dim)
        before = lax.ppermute(last, axis, up)
        after = lax.ppermute(first, axis, down)
        value = jnp.concatenate([before, value, after], axis=dim)
    return value


def entering(value, axis, join, neutral):
    place = lax.axis_index(axis)
    gathered = jax.tree.map(
        lambda a, kind: lax.all_gather(a.astype(kind), axis), value, (jnp.bfloat16, jnp.bfloat16)
    )
    state = jax.tree.map(lambda a, e: jnp.zeros_like(a) + jnp.asarray(e, a.dtype), value, neutral)

    def one(hop, state):
        return join(
            state,
            jax.tree.map(
                lambda a, own: lax.dynamic_index_in_dim(a, hop, 0, False).astype(own.dtype),
                gathered,
                value,
            ),
        )

    return lax.fori_loop(0, place, one, state)


def carried_in(value, axis, combine, identity):
    count, place = (lax.axis_size(axis), lax.axis_index(axis))
    everything = lax.all_gather(value.astype(jnp.bfloat16), axis)
    start = jnp.broadcast_to(jnp.asarray(identity, value.dtype), value.shape)

    def hop(k, before):
        at = count - 1 - k
        reached = at > place
        new = combine(before, everything[at].astype(value.dtype))
        return jnp.where(reached, new, before)

    return lax.fori_loop(0, count, hop, start)


def entering_2(value, axis, join, neutral, backward):
    count = lax.axis_size(axis)
    place = lax.axis_index(axis)
    ahead = count - 1 - place if backward else place
    gathered = jax.tree.map(
        lambda a, kind: lax.all_gather(a.astype(kind), axis),
        value,
        jax.tree.map(lambda a: jnp.bfloat16 if a.dtype == jnp.float32 else a.dtype, value),
    )
    state = jax.tree.map(lambda a, e: jnp.zeros_like(a) + jnp.asarray(e, a.dtype), value, neutral)

    def one(hop, state):
        source = count - 1 - hop if backward else hop
        return join(
            state,
            jax.tree.map(
                lambda a, own: lax.dynamic_index_in_dim(a, source, 0, False).astype(own.dtype),
                gathered,
                value,
            ),
        )

    return lax.fori_loop(0, ahead, one, state)


def shortened(value):

    def short(part):
        return part.astype(jnp.bfloat16) if part.dtype == jnp.float32 else part

    return jax.tree.map(short, value)


def sigmoid_linear(value):
    return value * jax.nn.sigmoid(value)


def sigmoid_slope(value):
    logistic = jax.nn.sigmoid(value)
    return logistic * (1.0 + value * (1.0 - logistic))


def add_tree(earlier, later):
    return jax.tree.map(jnp.add, earlier, later)


def mesa_block(queries, keys, values, ridge, state_kk, state_kv, valid):
    span = queries.shape[1]
    causal = jnp.tril(jnp.ones((span, span), queries.dtype))
    solution = jnp.zeros_like(queries)
    residue = queries
    direc = queries
    squares = jnp.sum(residue * residue, -1, keepdims=True)
    for step in range(ITERS):
        apply_inner = jnp.einsum("hcd,hed->hce", direc, keys, precision=HIGH) * causal
        image = jnp.einsum("hcd,hde->hce", direc, state_kk, precision=HIGH)
        image = image + jnp.einsum("hce,hed->hcd", apply_inner, keys, precision=HIGH)
        image = image + ridge[:, None, :] * direc
        alpha = squares / jnp.sum(direc * image, -1, keepdims=True)
        solution = solution + alpha * direc
        residue = residue - alpha * image
        if step + 1 < ITERS:
            fresh = jnp.sum(residue * residue, -1, keepdims=True)
            direc = residue + fresh / squares * direc
            squares = fresh
    inner = jnp.einsum("hcd,hed->hce", solution, keys, precision=HIGH) * causal
    mixed = jnp.einsum("hcd,hde->hce", solution, state_kv, precision=HIGH)
    mixed = mixed + jnp.einsum("hce,hed->hcd", inner, values, precision=HIGH)
    return mixed * valid[None, :, None]


def solve_blocks(queries, keys, values, ridge, state_kk, state_kv, valid):
    return jax.vmap(mesa_block, (0, 0, 0, None, 0, 0, 0))(
        queries, keys, values, ridge, state_kk, state_kv, valid
    )


def fetch_weights(weights):
    return (
        lax.all_gather(weights[0], "fsdp", axis=0, tiled=True),
        lax.all_gather(weights[1], "fsdp", axis=0, tiled=True),
        lax.all_gather(weights[2], "fsdp", axis=0, tiled=True),
        lax.all_gather(weights[3], "fsdp", axis=0, tiled=True),
        lax.all_gather(weights[4], "fsdp", axis=0, tiled=True),
        lax.all_gather(weights[5], "fsdp", axis=0, tiled=True),
        lax.all_gather(weights[6], "fsdp", axis=0, tiled=True),
        lax.all_gather(weights[7], "fsdp", axis=0, tiled=True),
    )


def spread_grads(grads):
    partial_sums = (
        lax.psum_scatter(
            grads[0].astype(jnp.bfloat16), "ctx", scatter_dimension=1, tiled=True
        ).astype(jnp.float32),
        lax.psum_scatter(
            grads[1].astype(jnp.bfloat16), "ctx", scatter_dimension=1, tiled=True
        ).astype(jnp.float32),
        lax.psum_scatter(
            grads[2].astype(jnp.bfloat16), "ctx", scatter_dimension=1, tiled=True
        ).astype(jnp.float32),
        lax.psum_scatter(
            grads[3].astype(jnp.bfloat16), "ctx", scatter_dimension=1, tiled=True
        ).astype(jnp.float32),
        lax.psum_scatter(
            grads[4].astype(jnp.bfloat16), "ctx", scatter_dimension=1, tiled=True
        ).astype(jnp.float32),
        lax.psum_scatter(
            grads[5].astype(jnp.bfloat16), "ctx", scatter_dimension=1, tiled=True
        ).astype(jnp.float32),
        lax.psum_scatter(
            grads[6].astype(jnp.bfloat16), "ctx", scatter_dimension=1, tiled=True
        ).astype(jnp.float32),
        lax.psum_scatter(
            grads[7].astype(jnp.bfloat16), "ctx", scatter_dimension=1, tiled=True
        ).astype(jnp.float32),
        lax.psum_scatter(
            grads[8].astype(jnp.bfloat16), "ctx", scatter_dimension=1, tiled=True
        ).astype(jnp.float32),
    )
    return (
        lax.psum_scatter(
            partial_sums[0].astype(jnp.bfloat16), "fsdp", scatter_dimension=1, tiled=True
        ).astype(jnp.float32),
        lax.psum_scatter(
            partial_sums[1].astype(jnp.bfloat16), "fsdp", scatter_dimension=1, tiled=True
        ).astype(jnp.float32),
        lax.psum_scatter(
            partial_sums[2].astype(jnp.bfloat16), "fsdp", scatter_dimension=1, tiled=True
        ).astype(jnp.float32),
        lax.psum_scatter(
            partial_sums[3].astype(jnp.bfloat16), "fsdp", scatter_dimension=1, tiled=True
        ).astype(jnp.float32),
        lax.psum_scatter(
            partial_sums[4].astype(jnp.bfloat16), "fsdp", scatter_dimension=1, tiled=True
        ).astype(jnp.float32),
        lax.psum_scatter(
            partial_sums[5].astype(jnp.bfloat16), "fsdp", scatter_dimension=1, tiled=True
        ).astype(jnp.float32),
        lax.psum_scatter(
            partial_sums[6].astype(jnp.bfloat16), "fsdp", scatter_dimension=1, tiled=True
        ).astype(jnp.float32),
        lax.psum_scatter(
            partial_sums[7].astype(jnp.bfloat16), "fsdp", scatter_dimension=1, tiled=True
        ).astype(jnp.float32),
        lax.psum_scatter(
            partial_sums[8].astype(jnp.bfloat16), "fsdp", scatter_dimension=1, tiled=True
        ).astype(jnp.float32),
    )


def matmul(left, right):
    return jnp.dot(left, right, preferred_element_type=jnp.float32)


def matmul_right_t(left, right):
    return jnp.einsum("tf,df->td", left, right, preferred_element_type=jnp.float32)


def matmul_left_t(left, right):
    return jnp.einsum("td,tf->df", left, right, preferred_element_type=jnp.float32)


def body(
    tokens,
    lengths,
    w_query,
    w_key,
    w_value,
    w_mixgate,
    w_output,
    w_ffgate,
    w_ffup,
    w_ffdown,
    conv_weight,
    norm_first,
    norm_second,
    ridge_log,
    out_grad,
):
    micro_count = tokens.shape[0]
    rows = tokens.shape[2]
    width = tokens.shape[3]
    kernel = conv_weight.shape[1]
    reach = kernel - 1
    span = C
    blocks = rows // span
    state_pairs = blocks // 2
    position = lax.axis_index("ctx")
    count = lax.axis_size("ctx")
    slot = jnp.arange(blocks)
    number = slot // 2 * 2 * count + jnp.where(slot % 2 == 0, position, 2 * count - 1 - position)
    seq_pos = number[:, None] * span + jnp.arange(span)[None, :]
    ridge = jnp.exp(ridge_log).reshape(HEAD_COUNT, HEAD_SIZE)
    taps = jnp.transpose(conv_weight, (1, 0, 2)).reshape(kernel, 3 * width)
    rim_zeros = jnp.zeros((1, reach, 3 * width), jnp.float32)
    state_zero = jnp.zeros((state_pairs, HEAD_COUNT, 2, HEAD_SIZE, HEAD_SIZE), jnp.float32)

    def heads(rows_in):
        return rows_in.reshape(blocks, span, HEAD_COUNT, HEAD_SIZE).transpose(0, 2, 1, 3)

    def unheads(blocks_in):
        return blocks_in.transpose(0, 2, 1, 3).reshape(rows, width)

    results = []
    input_grads = []
    shard_sums = None
    for micro in range(micro_count):
        (
            full_query,
            full_key,
            full_value,
            full_mixgate,
            full_output,
            full_ffgate,
            full_ffup,
            full_ffdown,
        ) = fetch_weights(
            (w_query, w_key, w_value, w_mixgate, w_output, w_ffgate, w_ffup, w_ffdown)
        )
        inputs = tokens[micro, 0].astype(jnp.float32)
        valid = (seq_pos < lengths[micro, 0]).astype(jnp.float32)
        mask = valid[:, None, :, None]
        first_scale = lax.rsqrt(jnp.mean(inputs * inputs, -1, keepdims=True) + EPS)
        normed = (inputs * first_scale * norm_first).astype(jnp.bfloat16)
        pre_query = matmul(normed, full_query)
        pre_key = matmul(normed, full_key)
        pre_value = matmul(normed, full_value)
        pre_gate = matmul(normed, full_mixgate)
        joined = jnp.concatenate([pre_query, pre_key, pre_value], -1).reshape(
            blocks, span, 3 * width
        )
        tails = joined[:, span - reach :].reshape(state_pairs, 2, reach, 3 * width)
        rims = jnp.concatenate([tails[:, 1], tails[:, 0]], 1)
        framed = extended_2(rims.astype(jnp.bfloat16), (("ctx", 1),), reach).astype(rims.dtype)
        earlier_second = jnp.concatenate([rim_zeros, tails[:-1, 1]], 0)
        before_first = jnp.where(position > 0, framed[:, :reach], earlier_second)
        before_second = jnp.where(position < count - 1, framed[:, 3 * reach :], tails[:, 0])
        before = jnp.stack([before_first, before_second], 1).reshape(blocks, reach, 3 * width)
        padded = jnp.concatenate([before, joined], 1)
        convolved = taps[0] * joined
        for lag in range(1, kernel):
            convolved = convolved + taps[lag] * padded[:, reach - lag : reach - lag + span]
        activated = sigmoid_linear(convolved).reshape(rows, 3 * width)
        act_query = heads(activated[:, :width])
        act_key = heads(activated[:, width : 2 * width])
        act_value = heads(activated[:, 2 * width :])
        query_scale = lax.rsqrt(jnp.sum(act_query * act_query, -1, keepdims=True) + EPS)
        key_scale = lax.rsqrt(jnp.sum(act_key * act_key, -1, keepdims=True) + EPS)
        queries = act_query * query_scale
        keys = act_key * key_scale * mask
        values = act_value * mask
        block_kk = jnp.einsum("jhcd,jhce->jhde", keys, keys, precision=HIGH)
        block_kv = jnp.einsum("jhcd,jhce->jhde", keys, values, precision=HIGH)
        totals = jnp.stack([block_kk, block_kv], 2).reshape(
            state_pairs, 2, HEAD_COUNT, 2, HEAD_SIZE, HEAD_SIZE
        )
        firsts = totals[:, 0]
        both = firsts + totals[:, 1]
        before_firsts, before_both = entering(
            (firsts, both), "ctx", add_tree, (state_zero, state_zero)
        )
        after_both = carried_in(both, "ctx", add_tree, state_zero)
        pair_totals = before_both + both + after_both
        earlier_pairs = jnp.cumsum(pair_totals, 0) - pair_totals
        prefix_first = earlier_pairs + before_firsts
        prefix_second = prefix_first + firsts + after_both
        prefix = jnp.stack([prefix_first, prefix_second], 1).reshape(
            blocks, HEAD_COUNT, 2, HEAD_SIZE, HEAD_SIZE
        )
        mixed, pullback_function = jax.vjp(
            partial(solve_blocks, valid=valid),
            queries,
            keys,
            values,
            ridge,
            prefix[:, :, 0],
            prefix[:, :, 1],
        )
        mixed_rows = unheads(mixed)
        gate_act = sigmoid_linear(pre_gate)
        gated = (mixed_rows * gate_act).astype(jnp.bfloat16)
        middle = inputs + matmul(gated, full_output)
        second_scale = lax.rsqrt(jnp.mean(middle * middle, -1, keepdims=True) + EPS)
        normed_two = (middle * second_scale * norm_second).astype(jnp.bfloat16)
        swish_pre = matmul(normed_two, full_ffgate)
        lift = matmul(normed_two, full_ffup)
        swish = sigmoid_linear(swish_pre)
        hidden = (swish * lift).astype(jnp.bfloat16)
        results.append((middle + matmul(hidden, full_ffdown)).astype(jnp.bfloat16))
        upstream = out_grad[micro, 0]
        grad_ffdown = matmul_left_t(hidden, upstream)
        grad_hidden = matmul_right_t(upstream, full_ffdown)
        grad_swish = (grad_hidden * lift * sigmoid_slope(swish_pre)).astype(jnp.bfloat16)
        grad_lift = (grad_hidden * swish).astype(jnp.bfloat16)
        grad_ffgate = matmul_left_t(normed_two, grad_swish)
        grad_ffup = matmul_left_t(normed_two, grad_lift)
        grad_two = matmul_right_t(grad_swish, full_ffgate) + matmul_right_t(grad_lift, full_ffup)
        scaled_two = grad_two * norm_second
        gain_second = jnp.sum(grad_two * middle * second_scale, 0)
        grad_middle = (
            second_scale * scaled_two
            - middle * second_scale**3 * jnp.mean(scaled_two * middle, -1, keepdims=True)
            + upstream.astype(jnp.float32)
        )
        grad_branch = grad_middle.astype(jnp.bfloat16)
        grad_output = matmul_left_t(gated, grad_branch)
        grad_gated = matmul_right_t(grad_branch, full_output)
        grad_mixed = grad_gated * gate_act
        grad_pregate = (grad_gated * mixed_rows * sigmoid_slope(pre_gate)).astype(jnp.bfloat16)
        grad_mixgate = matmul_left_t(normed, grad_pregate)
        (
            query_gradients,
            key_gradients,
            value_gradients,
            ridge_gradient,
            key_state_gradient,
            value_state_gradient,
        ) = pullback_function(heads(grad_mixed))
        returned_values = jnp.stack([key_state_gradient, value_state_gradient], 2).reshape(
            state_pairs, 2, HEAD_COUNT, 2, HEAD_SIZE, HEAD_SIZE
        )
        ret_second = returned_values[:, 1]
        ret_both = returned_values[:, 0] + ret_second
        low_second, low_both = entering_2(
            (ret_second, ret_both), "ctx", add_tree, (state_zero, state_zero), False
        )
        high_both = entering_2(ret_both, "ctx", add_tree, state_zero, True)
        pair_sums = low_both + ret_both + high_both
        later_pairs = jnp.sum(pair_sums, 0, keepdims=True) - jnp.cumsum(pair_sums, 0)
        into_second = later_pairs + low_second
        into_first = into_second + high_both + ret_second
        into = jnp.stack([into_first, into_second], 1).reshape(
            blocks, HEAD_COUNT, 2, HEAD_SIZE, HEAD_SIZE
        )
        into_kk = into[:, :, 0]
        into_kv = into[:, :, 1]
        key_gradients = key_gradients + jnp.einsum(
            "jhce,jhde->jhcd", keys, into_kk + jnp.swapaxes(into_kk, -1, -2), precision=HIGH
        )
        key_gradients = key_gradients + jnp.einsum(
            "jhce,jhde->jhcd", values, into_kv, precision=HIGH
        )
        value_gradients = value_gradients + jnp.einsum(
            "jhcd,jhde->jhce", keys, into_kv, precision=HIGH
        )
        key_gradients = key_gradients * mask
        value_gradients = value_gradients * mask
        grad_act_query = query_scale * query_gradients - act_query * query_scale**3 * jnp.sum(
            query_gradients * act_query, -1, keepdims=True
        )
        grad_act_key = key_scale * key_gradients - act_key * key_scale**3 * jnp.sum(
            key_gradients * act_key, -1, keepdims=True
        )
        grad_act = jnp.concatenate(
            [unheads(grad_act_query), unheads(grad_act_key), unheads(value_gradients)], -1
        )
        grad_conv = grad_act.reshape(blocks, span, 3 * width) * sigmoid_slope(convolved)
        leads = grad_conv[:, :reach].reshape(state_pairs, 2, reach, 3 * width)
        rims_back = jnp.concatenate([leads[:, 0], leads[:, 1]], 1)
        framed_back = extended_2(shortened(rims_back), (("ctx", 1),), reach).astype(rims_back.dtype)
        later_first = jnp.concatenate([leads[1:, 0], rim_zeros], 0)
        next_first = jnp.where(position < count - 1, framed_back[:, 3 * reach :], leads[:, 1])
        next_second = jnp.where(position > 0, framed_back[:, :reach], later_first)
        after = jnp.stack([next_first, next_second], 1).reshape(blocks, reach, 3 * width)
        extended = jnp.concatenate([grad_conv, after], 1)
        grad_joined = taps[0] * grad_conv
        tap_grads = [jnp.sum(grad_conv * joined, (0, 1))]
        for lag in range(1, kernel):
            grad_joined = grad_joined + taps[lag] * extended[:, lag : lag + span]
            tap_grads.append(
                jnp.sum(grad_conv * padded[:, reach - lag : reach - lag + span], (0, 1))
            )
        grad_taps = (
            jnp.stack(tap_grads, 0)
            .reshape(kernel, 3, width)
            .transpose(1, 0, 2)
            .reshape(3 * kernel, width)
        )
        grad_pre = grad_joined.reshape(rows, 3 * width).astype(jnp.bfloat16)
        grad_pre_query = grad_pre[:, :width]
        grad_pre_key = grad_pre[:, width : 2 * width]
        grad_pre_value = grad_pre[:, 2 * width :]
        grad_query = matmul_left_t(normed, grad_pre_query)
        grad_key = matmul_left_t(normed, grad_pre_key)
        grad_value = matmul_left_t(normed, grad_pre_value)
        grad_normed = (
            matmul_right_t(grad_pre_query, full_query)
            + matmul_right_t(grad_pre_key, full_key)
            + matmul_right_t(grad_pre_value, full_value)
            + matmul_right_t(grad_pregate, full_mixgate)
        )
        scaled_first = grad_normed * norm_first
        gain_first = jnp.sum(grad_normed * inputs * first_scale, 0)
        grad_inputs = (
            first_scale * scaled_first
            - inputs * first_scale**3 * jnp.mean(scaled_first * inputs, -1, keepdims=True)
            + grad_middle
        )
        input_grads.append(grad_inputs.astype(jnp.bfloat16))
        ridge_grad = (ridge_gradient * ridge).reshape(width)
        small = jnp.concatenate(
            [grad_taps, gain_first[None], gain_second[None], ridge_grad[None]], 0
        )
        grads = (
            grad_query,
            grad_key,
            grad_value,
            grad_mixgate,
            grad_output,
            grad_ffgate,
            grad_ffup,
            grad_ffdown,
            small,
        )
        shards = spread_grads(grads)
        shard_sums = shards if shard_sums is None else add_tree(shard_sums, shards)
    small_shard = shard_sums[8]
    conv_shard = small_shard[: 3 * kernel].reshape(3, kernel, small_shard.shape[1])
    result = jnp.stack(results, 0)[:, None]
    input_grad = jnp.stack(input_grads, 0)[:, None]
    return (
        result,
        input_grad,
        shard_sums[0],
        shard_sums[1],
        shard_sums[2],
        shard_sums[3],
        shard_sums[4],
        shard_sums[5],
        shard_sums[6],
        shard_sums[7],
        conv_shard,
        small_shard[3 * kernel],
        small_shard[3 * kernel + 1],
        small_shard[3 * kernel + 2],
    )


def solution(mesh):
    return jax.shard_map(
        body,
        mesh=mesh,
        in_specs=(
            P(None, "fsdp", "ctx", None),
            P(None, "fsdp"),
            P("fsdp", None),
            P("fsdp", None),
            P("fsdp", None),
            P("fsdp", None),
            P("fsdp", None),
            P("fsdp", None),
            P("fsdp", None),
            P("fsdp", None),
            P(),
            P(),
            P(),
            P(),
            P(None, "fsdp", "ctx", None),
        ),
        out_specs=(
            P(None, "fsdp", "ctx", None),
            P(None, "fsdp", "ctx", None),
            P(None, ("ctx", "fsdp")),
            P(None, ("ctx", "fsdp")),
            P(None, ("ctx", "fsdp")),
            P(None, ("ctx", "fsdp")),
            P(None, ("ctx", "fsdp")),
            P(None, ("ctx", "fsdp")),
            P(None, ("ctx", "fsdp")),
            P(None, ("ctx", "fsdp")),
            P(None, None, ("ctx", "fsdp")),
            P(("ctx", "fsdp")),
            P(("ctx", "fsdp")),
            P(("ctx", "fsdp")),
        ),
        check_vma=False,
    )
```

profile of v0, /device:TPU:0, one launch (start us, length us, event | category | flops | bytes accessed | tf_op | source)
XLA Modules:
  0.0 2947.9 jit_solution(14921725145607181712)
XLA Ops:
  218.4 54.2 %all-gather.23.cloned.1.call-done = bf16[8,1,8,2,128,128]{5,4,3,2,1,0:T(8,128)(2,1)} async-done(((bf16[1,1,8,2,128,128]{5,4,3,2,1,0:T(8,128)(2,1)}), bf16[8,1,8,2,128,128]{5,4,3,2,1,0:T(8,128)(2,1)}) %all-gather.23.cloned.1.call-update) | async-done | bytes 4194320 | tf_op jit(solution)/shard_map/all_gather | solution.py:34
  282.1 64.1 %all-gather.39.cloned.1.call-done = bf16[8,1,8,2,128,128]{5,4,3,2,1,0:T(8,128)(2,1)} async-done(((bf16[1,1,8,2,128,128]{5,4,3,2,1,0:T(8,128)(2,1)}), bf16[8,1,8,2,128,128]{5,4,3,2,1,0:T(8,128)(2,1)}) %all-gather.39.cloned.1.call-update) | async-done | bytes 4194320 | tf_op jit(solution)/shard_map/all_gather | solution.py:34
  346.2 73.8 %all-gather.37.cloned.1.call-done = bf16[8,1,8,2,128,128]{5,4,3,2,1,0:T(8,128)(2,1)} async-done(((bf16[1,1,8,2,128,128]{5,4,3,2,1,0:T(8,128)(2,1)}), bf16[8,1,8,2,128,128]{5,4,3,2,1,0:T(8,128)(2,1)}) %all-gather.37.cloned.1.call-update) | async-done | bytes 4194320 | tf_op jit(solution)/shard_map/all_gather | solution.py:34
  482.9 28.6 all-gather.31.cloned.1.call-done
  517.6 39.0 %all-gather.33.cloned.1.call-done = bf16[1024,2816]{1,0:T(8,128)(2,1)} async-done(((bf16[256,2816]{1,0:T(8,128)(2,1)}), bf16[1024,2816]{1,0:T(8,128)(2,1)}) %all-gather.33.cloned.1.call-update) | async-done | bytes 5767184 | tf_op jit(solution)/shard_map/all_gather | solution.py:150
  562.6 38.8 %all-gather.35.cloned.1.call-done = bf16[2816,1024]{1,0:T(8,128)(2,1)} async-done(((bf16[704,1024]{1,0:T(8,128)(2,1)}), bf16[2816,1024]{1,0:T(8,128)(2,1)}) %all-gather.35.cloned.1.call-update) | async-done | bytes 5767184 | tf_op jit(solution)/shard_map/all_gather | solution.py:151
  833.1 27.9 all-gather.41.cloned.1.call-done
  944.2 65.1 %all-gather.45.cloned.1.call-done = bf16[8,1,8,2,128,128]{5,4,3,2,1,0:T(8,128)(2,1)} async-done(((bf16[1,1,8,2,128,128]{5,4,3,2,1,0:T(8,128)(2,1)}), bf16[8,1,8,2,128,128]{5,4,3,2,1,0:T(8,128)(2,1)}) %all-gather.45.cloned.1.call-update) | async-done | bytes 4194320 | tf_op jit(solution)/shard_map/all_gather | solution.py:70
  1165.0 54.3 %reduce-scatter.145.cloned.1.call-done = bf16[128,1024]{1,0:T(8,128)(2,1)} async-done(((bf16[1024,1024]{1,0:T(8,128)(2,1)}), bf16[128,1024]{1,0:T(8,128)(2,1)}) %reduce-scatter.145.cloned.1.call-update) | async-done | bytes 262160
  1219.4 70.0 %reduce-scatter.141.cloned.1.call-done = bf16[128,1024]{1,0:T(8,128)(2,1)} async-done(((bf16[1024,1024]{1,0:T(8,128)(2,1)}), bf16[128,1024]{1,0:T(8,128)(2,1)}) %reduce-scatter.141.cloned.1.call-update) | async-done | bytes 262160
  1295.1 58.5 %reduce-scatter.161.cloned.1.call-done = bf16[128,15]{1,0:T(8,128)(2,1)} async-done(((bf16[1024,15]{1,0:T(8,128)(2,1)}), bf16[128,15]{1,0:T(8,128)(2,1)}) %reduce-scatter.161.cloned.1.call-update) | async-done | bytes 3856
  1353.8 63.9 %reduce-scatter.157.cloned.1.call-done = bf16[128,15]{1,0:T(8,128)(2,1)} async-done(((bf16[1024,15]{1,0:T(8,128)(2,1)}), bf16[128,15]{1,0:T(8,128)(2,1)}) %reduce-scatter.157.cloned.1.call-update) | async-done | bytes 3856
  1423.4 64.5 %reduce-scatter.113.cloned.1.call-done = bf16[128,1024]{1,0:T(8,128)(2,1)} async-done(((bf16[1024,1024]{1,0:T(8,128)(2,1)}), bf16[128,1024]{1,0:T(8,128)(2,1)}) %reduce-scatter.113.cloned.1.call-update) | async-done | bytes 262160
  1488.0 70.0 %reduce-scatter.109.cloned.1.call-done = bf16[128,1024]{1,0:T(8,128)(2,1)} async-done(((bf16[1024,1024]{1,0:T(8,128)(2,1)}), bf16[128,1024]{1,0:T(8,128)(2,1)}) %reduce-scatter.109.cloned.1.call-update) | async-done | bytes 262160
  1558.0 70.1 %reduce-scatter.121.cloned.1.call-done = bf16[128,1024]{1,0:T(8,128)(2,1)} async-done(((bf16[1024,1024]{1,0:T(8,128)(2,1)}), bf16[128,1024]{1,0:T(8,128)(2,1)}) %reduce-scatter.121.cloned.1.call-update) | async-done | bytes 262160
  1628.2 70.0 %reduce-scatter.117.cloned.1.call-done = bf16[128,1024]{1,0:T(8,128)(2,1)} async-done(((bf16[1024,1024]{1,0:T(8,128)(2,1)}), bf16[128,1024]{1,0:T(8,128)(2,1)}) %reduce-scatter.117.cloned.1.call-update) | async-done | bytes 262160
  1698.3 70.2 %reduce-scatter.129.cloned.1.call-done = bf16[128,1024]{1,0:T(8,128)(2,1)} async-done(((bf16[1024,1024]{1,0:T(8,128)(2,1)}), bf16[128,1024]{1,0:T(8,128)(2,1)}) %reduce-scatter.129.cloned.1.call-update) | async-done | bytes 262160
  1768.6 70.4 %reduce-scatter.125.cloned.1.call-done = bf16[128,1024]{1,0:T(8,128)(2,1)} async-done(((bf16[1024,1024]{1,0:T(8,128)(2,1)}), bf16[128,1024]{1,0:T(8,128)(2,1)}) %reduce-scatter.125.cloned.1.call-update) | async-done | bytes 262160
  1839.0 112.6 %reduce-scatter.153.cloned.1.call-done = bf16[128,2816]{1,0:T(8,128)(2,1)} async-done(((bf16[1024,2816]{1,0:T(8,128)(2,1)}), bf16[128,2816]{1,0:T(8,128)(2,1)}) %reduce-scatter.153.cloned.1.call-update) | async-done | bytes 720912
  1951.7 113.2 %reduce-scatter.149.cloned.1.call-done = bf16[128,2816]{1,0:T(8,128)(2,1)} async-done(((bf16[1024,2816]{1,0:T(8,128)(2,1)}), bf16[128,2816]{1,0:T(8,128)(2,1)}) %reduce-scatter.149.cloned.1.call-update) | async-done | bytes 720912
  2065.0 113.4 %reduce-scatter.97.cloned.1.call-done = bf16[1024,352]{0,1:T(8,128)(2,1)} async-done(((bf16[1024,2816]{0,1:T(8,128)(2,1)}), bf16[1024,352]{0,1:T(8,128)(2,1)}) %reduce-scatter.97.cloned.1.call-update) | async-done | bytes 720912 | tf_op jit(solution)/shard_map/reduce_scatter | solution.py:172
  2178.4 113.4 %reduce-scatter.93.cloned.1.call-done = bf16[1024,352]{0,1:T(8,128)(2,1)} async-done(((bf16[1024,2816]{0,1:T(8,128)(2,1)}), bf16[1024,352]{0,1:T(8,128)(2,1)}) %reduce-scatter.93.cloned.1.call-update) | async-done | bytes 720912 | tf_op jit(solution)/shard_map/reduce_scatter | solution.py:172
  2385.2 109.9 %reduce-scatter.105.cloned.1.call-done = bf16[1024,352]{0,1:T(8,128)(2,1)} async-done(((bf16[1024,2816]{0,1:T(8,128)(2,1)}), bf16[1024,352]{0,1:T(8,128)(2,1)}) %reduce-scatter.105.cloned.1.call-update) | async-done | bytes 720912 | tf_op jit(solution)/shard_map/reduce_scatter | solution.py:175
  2540.3 111.7 %reduce-scatter.101.cloned.1.call-done = bf16[1024,352]{0,1:T(8,128)(2,1)} async-done(((bf16[1024,2816]{0,1:T(8,128)(2,1)}), bf16[1024,352]{0,1:T(8,128)(2,1)}) %reduce-scatter.101.cloned.1.call-update) | async-done | bytes 720912 | tf_op jit(solution)/shard_map/reduce_scatter | solution.py:175
  (928 shorter events, 1259.9 us)
Async XLA Ops:
  156.3 667.5 %all-gather.43.cloned.1.call-start = ((), (), s32[]{:S(2)}) async-start(), calls=%async_computation.49 | async-start | bytes 4718592 | tf_op jit(solution)/shard_map/all_gather | solution.py:70
  1114.9 724.0 %reduce-scatter.125.cloned.1.call-start = ((), (), s32[]{:S(2)}) async-start(), calls=%async_computation.68 | async-start | bytes 2359296
  1122.3 829.4 %reduce-scatter.153.cloned.1.call-start = ((), (), s32[]{:S(2)}) async-start(), calls=%async_computation.82 | async-start | bytes 6488064
  1136.2 928.6 %reduce-scatter.149.cloned.1.call-start = ((), (), s32[]{:S(2)}) async-start(), calls=%async_computation.80 | async-start | bytes 6488064
  1150.3 1028.1 %reduce-scatter.97.cloned.1.call-start = ((), (), s32[]{:S(2)}) async-start(), calls=%async_computation.54 | async-start | bytes 6488064 | tf_op jit(solution)/shard_map/reduce_scatter | solution.py:172
  1156.8 1134.9 %reduce-scatter.93.cloned.1.call-start = ((), (), s32[]{:S(2)}) async-start(), calls=%async_computation.52 | async-start | bytes 6488064 | tf_op jit(solution)/shard_map/reduce_scatter | solution.py:172
  1163.7 1150.2 %reduce-scatter.139.cloned.1.call-start = ((), (), s32[]{:S(2)}) async-start(), calls=%async_computation.75 | async-start | bytes 327680
  1164.2 1172.4 %reduce-scatter.135.cloned.1.call-start = ((), (), s32[]{:S(2)}) async-start(), calls=%async_computation.73 | async-start | bytes 327680
  1165.0 1194.1 %reduce-scatter.147.cloned.1.call-start = ((), (), s32[]{:S(2)}) async-start(), calls=%async_computation.79 | async-start | bytes 327680
  1219.3 1162.3 %reduce-scatter.143.cloned.1.call-start = ((), (), s32[]{:S(2)}) async-start(), calls=%async_computation.77 | async-start | bytes 327680
  1289.4 1205.7 %reduce-scatter.105.cloned.1.call-start = ((), (), s32[]{:S(2)}) async-start(), calls=%async_computation.58 | async-start | bytes 6488064 | tf_op jit(solution)/shard_map/reduce_scatter | solution.py:175
  1295.0 1221.7 %reduce-scatter.163.cloned.1.call-start = ((), (), s32[]{:S(2)}) async-start(), calls=%async_computation.87 | async-start | bytes 40960
  1353.6 1184.8 %reduce-scatter.159.cloned.1.call-start = ((), (), s32[]{:S(2)}) async-start(), calls=%async_computation.85 | async-start | bytes 40960
  1417.7 1234.4 %reduce-scatter.101.cloned.1.call-start = ((), (), s32[]{:S(2)}) async-start(), calls=%async_computation.56 | async-start | bytes 6488064 | tf_op jit(solution)/shard_map/reduce_scatter | solution.py:175
  1423.3 1251.1 %reduce-scatter.115.cloned.1.call-start = ((), (), s32[]{:S(2)}) async-start(), calls=%async_computation.63 | async-start | bytes 327680
  1487.9 1209.1 %reduce-scatter.111.cloned.1.call-start = ((), (), s32[]{:S(2)}) async-start(), calls=%async_computation.61 | async-start | bytes 327680
  1558.0 1161.4 %reduce-scatter.123.cloned.1.call-start = ((), (), s32[]{:S(2)}) async-start(), calls=%async_computation.67 | async-start | bytes 327680
  1628.2 1113.9 %reduce-scatter.119.cloned.1.call-start = ((), (), s32[]{:S(2)}) async-start(), calls=%async_computation.65 | async-start | bytes 327680
  1698.3 1066.2 %reduce-scatter.131.cloned.1.call-start = ((), (), s32[]{:S(2)}) async-start(), calls=%async_computation.71 | async-start | bytes 327680
  1768.6 1018.4 %reduce-scatter.127.cloned.1.call-start = ((), (), s32[]{:S(2)}) async-start(), calls=%async_computation.69 | async-start | bytes 327680
  1839.0 973.2 %reduce-scatter.155.cloned.1.call-start = ((), (), s32[]{:S(2)}) async-start(), calls=%async_computation.83 | async-start | bytes 901120
  1951.6 886.0 %reduce-scatter.151.cloned.1.call-start = ((), (), s32[]{:S(2)}) async-start(), calls=%async_computation.81 | async-start | bytes 901120
  2064.9 798.0 %reduce-scatter.99.cloned.1.call-start = ((), (), s32[]{:S(2)}) async-start(), calls=%async_computation.55 | async-start | bytes 901120 | tf_op jit(solution)/shard_map/reduce_scatter | solution.py:201
  2178.3 710.2 %reduce-scatter.95.cloned.1.call-start = ((), (), s32[]{:S(2)}) async-start(), calls=%async_computation.53 | async-start | bytes 901120 | tf_op jit(solution)/shard_map/reduce_scatter | solution.py:201
  (236 other events, 13348.0 us)
Sparse Core Ops, SparseCore 0:
  123.2 75.6 all-gather.24
  200.9 71.6 all-gather.22
  274.5 71.6 all-gather.38
  348.4 71.6 all-gather.36
  713.8 73.3 all-gather.42
  789.2 71.6 all-gather.40
  862.9 71.9 all-gather.46
  936.9 72.3 all-gather.44
  1012.7 66.5 reduce-scatter.136
  1082.6 66.4 reduce-scatter.132
  1152.7 66.6 reduce-scatter.144
  1222.7 66.6 reduce-scatter.140
  1421.2 66.6 reduce-scatter.112
  1491.3 66.6 reduce-scatter.108
  1561.5 66.6 reduce-scatter.120
  1631.6 66.6 reduce-scatter.116
  1701.6 66.8 reduce-scatter.128
  1772.1 66.8 reduce-scatter.124
  1842.6 108.9 reduce-scatter.152
  1955.1 109.7 reduce-scatter.148
  2068.5 109.7 reduce-scatter.96
  2182.0 109.7 reduce-scatter.92
  2385.1 109.9 reduce-scatter.104
  2542.1 109.9 reduce-scatter.100
  (28 shorter events, 738.4 us)
where the time goes:
time: 2960 us; the launch traced here: 2950 us
  waiting for transfers between devices  2230 us (75%)
  matrix products  331 us (11%)
  local copies, waits for them, and re-layouts  180 us (6%)
  other arithmetic  141 us (5%)
  starting transfers between devices  44.5 us (2%)
    unnamed x80, waiting for transfers between devices  1180 us
    reduce_scatter x2, waiting for transfers between devices, spread_grads(): lax.psum_scatter(grads[5].astype(jnp.bfloat16), 'ctx', scatter_dimension=...  227 us
    reduce_scatter x2, waiting for transfers between devices, spread_grads(): lax.psum_scatter(grads[6].astype(jnp.bfloat16), 'ctx', scatter_dimension=...  222 us
    all_gather x4, waiting for transfers between devices, entering(): lax.all_gather(a.astype(kind), axis)  216 us
    all_gather x4, waiting for transfers between devices, entering_2(): lax.all_gather(a.astype(kind), axis)  121 us
    unnamed x444, local copies, waits for them, and re-layouts  114 us
    dot_general x16, matrix products, matmul_left_t(): jnp.einsum('td,tf->df', left, right, preferred_element_type=jnp.float32)  65.2 us
  transfers between devices with their start and end apart: 60, of which 48 were waited for; matrix products, arithmetic and copies ran while one was open for 17% of the time, Pallas kernels for 0%

commit v1 on v0

v1 whole, which is shorter than its diff:
```python
from functools import partial

import jax
import jax.numpy as jnp
from jax import lax
from jax.experimental import pallas as pl
from jax.experimental.pallas import tpu as pltpu
from jax.sharding import PartitionSpec as P

HEAD_COUNT = 8
HEAD_SIZE = 128
C = 128
EPS = 1e-06
GROUP = 4
PAD = 8
BF = jnp.bfloat16
F32 = jnp.float32
VMEM_BYTES = 56 * 1024 * 1024


def nn(a, b):
    return lax.dot_general(a, b, (((1,), (0,)), ((), ())), preferred_element_type=F32)


def nt(a, b):
    return lax.dot_general(a, b, (((1,), (1,)), ((), ())), preferred_element_type=F32)


def tn(a, b):
    return lax.dot_general(a, b, (((0,), (0,)), ((), ())), preferred_element_type=F32)


def silu(v):
    return v * jax.nn.sigmoid(v)


def slope(v):
    s = jax.nn.sigmoid(v)
    return s * (1.0 + v * (1.0 - s))


def rowsum(v):
    return jnp.sum(v, -1, keepdims=True)


def place_of(step, count):
    per_half = count // GROUP
    pair = step // (2 * per_half)
    rest = step % (2 * per_half)
    first = rest < per_half
    group = jnp.where(first, rest, 2 * per_half - 1 - rest)
    return group, pair * 2 + jnp.where(first, 0, 1), first


def causal_mask():
    rows = lax.broadcasted_iota(jnp.int32, (C, C), 0)
    cols = lax.broadcasted_iota(jnp.int32, (C, C), 1)
    return rows >= cols


def valid_rows(step, length):
    pos = step * (GROUP * C) + lax.broadcasted_iota(jnp.int32, (GROUP * C, 1), 0)
    return (pos < length).astype(F32)


def solve(q, k, kb, skk, ridge, tri):
    system = jnp.concatenate([kb, skk], 0)
    qb = q.astype(BF)
    inner0 = jnp.where(tri, nt(qb, kb), 0.0)
    i0 = nn(jnp.concatenate([inner0.astype(BF), qb], 1), system) + ridge * q
    rr0 = rowsum(q * q)
    p0 = rowsum(q * i0)
    a0 = rr0 / p0
    r1 = q - a0 * i0
    f = rowsum(r1 * r1)
    b = f / rr0
    d1 = r1 + b * q
    db = d1.astype(BF)
    inner1 = jnp.where(tri, nt(db, kb), 0.0)
    i1 = nn(jnp.concatenate([inner1.astype(BF), db], 1), system) + ridge * d1
    p1 = rowsum(d1 * i1)
    a1 = f / p1
    s2 = a0 * q + a1 * d1
    return system, qb, inner0, i0, rr0, p0, a0, r1, f, b, d1, inner1, i1, p1, a1, s2


def forward_kernel(
    count, len_ref, x_ref, w_ref, taps_ref, ridge_ref,
    gated_ref, pre_ref, mixed_ref, states_ref,
    padded, q_s, k_s, v_s, skk, skv,
):
    micro, step = pl.program_id(0), pl.program_id(1)
    _, _, first = place_of(step, count)
    span = GROUP * C

    @pl.when(step == 0)
    def _():
        padded[0:PAD, :] = jnp.zeros((PAD, 3 * HEAD_SIZE), F32)
        skk[...] = jnp.zeros_like(skk)
        skv[...] = jnp.zeros_like(skv)

    pre = nn(x_ref[...].reshape(span, x_ref.shape[-1]), w_ref[...])
    pre_ref[...] = pre.reshape(pre_ref.shape)
    for j in range(GROUP):
        jj = jnp.where(first, j, GROUP - 1 - j)
        padded[PAD + j * C : PAD + (j + 1) * C, :] = pre_ref[jj, 0, 0, :, : 3 * HEAD_SIZE]
    conv = taps_ref[0:1, :] * padded[PAD : PAD + span, :]
    for lag in range(1, 4):
        conv = conv + taps_ref[lag : lag + 1, :] * padded[PAD - lag : PAD - lag + span, :]
    padded[0:PAD, :] = padded[span : span + PAD, :]
    act = silu(conv)
    valid = valid_rows(step, len_ref[micro])
    act_q = act[:, :HEAD_SIZE]
    act_k = act[:, HEAD_SIZE : 2 * HEAD_SIZE]
    q_s[...] = act_q * lax.rsqrt(rowsum(act_q * act_q) + EPS)
    k_s[...] = act_k * (lax.rsqrt(rowsum(act_k * act_k) + EPS) * valid)
    v_s[...] = act[:, 2 * HEAD_SIZE :] * valid
    tri = causal_mask()
    ridge = ridge_ref[...]
    for j in range(GROUP):
        jj = jnp.where(first, j, GROUP - 1 - j)
        rows = slice(j * C, (j + 1) * C)
        k = k_s[rows, :]
        kb = k.astype(BF)
        vb = v_s[rows, :].astype(BF)
        kk_now = skk[...]
        kv_now = skv[...]
        states_ref[jj, 0, 0, 0] = kk_now
        states_ref[jj, 0, 0, 1] = kv_now
        s2 = solve(q_s[rows, :], k, kb, kk_now.astype(BF), ridge, tri)[-1]
        sb = s2.astype(BF)
        p = jnp.where(tri, nt(sb, kb), 0.0)
        mixed = nn(
            jnp.concatenate([p.astype(BF), sb], 1),
            jnp.concatenate([vb, kv_now.astype(BF)], 0),
        )
        mixed = mixed * valid[rows, :]
        mixed_ref[jj, 0, 0] = mixed
        gate = pre_ref[jj, 0, 0, :, 3 * HEAD_SIZE :]
        gated_ref[jj, 0, 0] = (mixed * silu(gate)).astype(BF)
        skk[...] = kk_now + tn(kb, kb)
        skv[...] = kv_now + tn(kb, vb)


def attention_forward(lengths, x, w, taps, ridge):
    count, micros, slots = x.shape[:3]
    width = x.shape[-1]
    steps = count * slots // GROUP

    def at(m, s):
        group, slot, _ = place_of(s, count)
        return (group, m, slot, 0, 0)

    def at_state(m, s):
        group, slot, _ = place_of(s, count)
        return (group, m, slot, 0, 0, 0)

    def block(columns):
        return pl.BlockSpec((GROUP, 1, 1, C, columns), at)

    whole = lambda shape: pl.BlockSpec(shape, lambda m, s: (0,) * len(shape))
    lead = (count, micros, slots, C)
    return pl.pallas_call(
        partial(forward_kernel, count),
        grid=(micros, steps),
        in_specs=[
            pl.BlockSpec(memory_space=pltpu.SMEM),
            block(width),
            whole(w.shape),
            whole(taps.shape),
            whole(ridge.shape),
        ],
        out_specs=[
            block(HEAD_SIZE),
            block(4 * HEAD_SIZE),
            block(HEAD_SIZE),
            pl.BlockSpec((GROUP, 1, 1, 2, HEAD_SIZE, HEAD_SIZE), at_state),
        ],
        out_shape=[
            jax.ShapeDtypeStruct((*lead, HEAD_SIZE), BF),
            jax.ShapeDtypeStruct((*lead, 4 * HEAD_SIZE), F32),
            jax.ShapeDtypeStruct((*lead, HEAD_SIZE), F32),
            jax.ShapeDtypeStruct((count, micros, slots, 2, HEAD_SIZE, HEAD_SIZE), F32),
        ],
        scratch_shapes=[
            pltpu.VMEM((GROUP * C + PAD, 3 * HEAD_SIZE), F32),
            pltpu.VMEM((GROUP * C, HEAD_SIZE), F32),
            pltpu.VMEM((GROUP * C, HEAD_SIZE), F32),
            pltpu.VMEM((GROUP * C, HEAD_SIZE), F32),
            pltpu.VMEM((HEAD_SIZE, HEAD_SIZE), F32),
            pltpu.VMEM((HEAD_SIZE, HEAD_SIZE), F32),
        ],
        compiler_params=pltpu.CompilerParams(vmem_limit_bytes=VMEM_BYTES),
        cost_estimate=pl.CostEstimate(
            flops=2 * count * micros * slots * C * (width * 512 + 11 * C * C),
            bytes_accessed=count * micros * slots * C * (2 * width + 4096),
            transcendentals=0,
        ),
        name="attn_forward",
    )(lengths, x, w, taps, ridge)


def backward_kernel(
    count, steps, len_ref, x_ref, g_ref, pre_ref, tail_ref, mixed_ref, states_ref, taps_ref, ridge_ref,
    dpre_ref, dw_ref, dtaps_ref, dridge_ref,
    padded, conv_s, act_s, q_s, k_s, dq_s, dk_s, dv_s, ext, gsum, hsum,
):
    micro, turn = pl.program_id(0), pl.program_id(1)
    step = steps - 1 - turn
    _, _, first = place_of(step, count)
    span = GROUP * C

    @pl.when(turn == 0)
    def _():
        ext[span : span + PAD, :] = jnp.zeros((PAD, 3 * HEAD_SIZE), F32)
        gsum[...] = jnp.zeros_like(gsum)
        hsum[...] = jnp.zeros_like(hsum)

    @pl.when((turn == 0) & (micro == 0))
    def _():
        dw_ref[...] = jnp.zeros_like(dw_ref)
        dtaps_ref[...] = jnp.zeros_like(dtaps_ref)
        dridge_ref[...] = jnp.zeros_like(dridge_ref)

    keep = jnp.where(step > 0, 1.0, 0.0)
    padded[0:PAD, :] = tail_ref[0, 0, 0, :, : 3 * HEAD_SIZE] * keep
    for j in range(GROUP):
        jj = jnp.where(first, j, GROUP - 1 - j)
        padded[PAD + j * C : PAD + (j + 1) * C, :] = pre_ref[jj, 0, 0, :, : 3 * HEAD_SIZE]
    conv = taps_ref[0:1, :] * padded[PAD : PAD + span, :]
    for lag in range(1, 4):
        conv = conv + taps_ref[lag : lag + 1, :] * padded[PAD - lag : PAD - lag + span, :]
    conv_s[...] = conv
    act = silu(conv)
    act_s[...] = act
    valid = valid_rows(step, len_ref[micro])
    act_q = act[:, :HEAD_SIZE]
    act_k = act[:, HEAD_SIZE : 2 * HEAD_SIZE]
    scale_q = lax.rsqrt(rowsum(act_q * act_q) + EPS)
    scale_k = lax.rsqrt(rowsum(act_k * act_k) + EPS)
    q_s[...] = act_q * scale_q
    k_s[...] = act_k * (scale_k * valid)
    tri = causal_mask()
    ridge = ridge_ref[...]
    ridge_total = jnp.zeros((1, HEAD_SIZE), F32)
    for j in reversed(range(GROUP)):
        jj = jnp.where(first, j, GROUP - 1 - j)
        rows = slice(j * C, (j + 1) * C)
        q = q_s[rows, :]
        k = k_s[rows, :]
        kb = k.astype(BF)
        vb = (act_s[rows, 2 * HEAD_SIZE :] * valid[rows, :]).astype(BF)
        skk = states_ref[jj, 0, 0, 0].astype(BF)
        skv = states_ref[jj, 0, 0, 1].astype(BF)
        system, qb, inner0, i0, rr0, p0, a0, r1, f, b, d1, inner1, i1, p1, a1, s2 = solve(
            q, k, kb, skk, ridge, tri
        )
        gate = pre_ref[jj, 0, 0, :, 3 * HEAD_SIZE :]
        d_gated = g_ref[jj, 0, 0].astype(F32)
        dpre_ref[jj, 0, 0, :, 3 * HEAD_SIZE :] = (
            d_gated * mixed_ref[jj, 0, 0] * slope(gate)
        ).astype(BF)
        g = (d_gated * silu(gate) * valid[rows, :]).astype(BF)
        sb = s2.astype(BF)
        p = jnp.where(tri, nt(sb, kb), 0.0)
        back = jnp.where(tri, nt(g, vb), 0.0)
        backb = back.astype(BF)
        ds = nn(backb, kb) + nt(g, skv)
        da1 = rowsum(ds * d1)
        df = da1 / p1
        dp1 = -df * a1
        dd1 = a1 * ds + (2.0 * dp1) * i1
        dbeta = rowsum(dd1 * q)
        inv_rr = 1.0 / rr0
        df = df + dbeta * inv_rr
        drr = -dbeta * b * inv_rr
        dr1 = dd1 + (2.0 * df) * r1
        da0 = rowsum(ds * q - dr1 * i0)
        da0p = da0 / p0
        drr = drr + da0p
        dp0 = -da0p * a0
        drb = dr1.astype(BF)
        innerr = jnp.where(tri, nt(drb, kb), 0.0)
        adr = nn(jnp.concatenate([innerr.astype(BF), drb], 1), system) + ridge * dr1
        dd0 = b * dd1 + a0 * ds + (2.0 * dp0) * i0 - a0 * adr
        di0 = dp0 * q - a0 * dr1
        dq_s[rows, :] = dr1 + dd0 + (2.0 * drr) * q
        wd1 = (2.0 * dp1) * d1
        ridge_total = ridge_total + jnp.sum(0.5 * wd1 * d1 + di0 * q, 0, keepdims=True)
        inneri = dp0 * inner0 - a0 * innerr
        di0b = di0.astype(BF)
        d1b = d1.astype(BF)
        wd1b = wd1.astype(BF)
        left = jnp.concatenate(
            [backb, inner1.astype(BF), inner0.astype(BF), inneri.astype(BF)], 0
        )
        right = jnp.concatenate([sb, wd1b, di0b, qb], 0)
        g_now = gsum[...]
        h_now = hsum[...]
        hb = h_now.astype(BF)
        dk_s[rows, :] = tn(left, right) + nn(kb, g_now.astype(BF)) + nt(vb, hb)
        both = tn(jnp.concatenate([p.astype(BF), sb], 1), g)
        dv_s[rows, :] = both[:C] + nn(kb, hb)
        hsum[...] = h_now + both[C:]
        gsum[...] = g_now + tn(
            jnp.concatenate([d1b, di0b, qb], 0), jnp.concatenate([wd1b, qb, di0b], 0)
        )
    dridge_ref[...] += ridge_total
    act = act_s[...]
    act_q = act[:, :HEAD_SIZE]
    act_k = act[:, HEAD_SIZE : 2 * HEAD_SIZE]
    dq = dq_s[...]
    dk = dk_s[...] * valid
    d_act_q = scale_q * dq - act_q * (scale_q * scale_q * scale_q * rowsum(dq * act_q))
    d_act_k = scale_k * dk - act_k * (scale_k * scale_k * scale_k * rowsum(dk * act_k))
    d_act = jnp.concatenate([d_act_q, d_act_k, dv_s[...] * valid], 1)
    ext[0:span, :] = d_act * slope(conv_s[...])
    now = padded[PAD : PAD + span, :]
    shifted = ext[0:span, :]
    d_pre = taps_ref[0:1, :] * shifted
    dtaps_ref[0:1, :] += jnp.sum(shifted * now, 0, keepdims=True)
    for lag in range(1, 4):
        shifted = ext[lag : lag + span, :]
        d_pre = d_pre + taps_ref[lag : lag + 1, :] * shifted
        dtaps_ref[lag : lag + 1, :] += jnp.sum(shifted * now, 0, keepdims=True)
    ext[span : span + PAD, :] = ext[0:PAD, :]
    d_pre = d_pre.astype(BF)
    for j in range(GROUP):
        jj = jnp.where(first, j, GROUP - 1 - j)
        dpre_ref[jj, 0, 0, :, : 3 * HEAD_SIZE] = d_pre[j * C : (j + 1) * C, :]
    dw_ref[...] += tn(
        dpre_ref[...].reshape(span, 4 * HEAD_SIZE), x_ref[...].reshape(span, x_ref.shape[-1])
    )


def attention_backward(lengths, x, d_gated, pre, mixed, states, taps, ridge):
    count, micros, slots = x.shape[:3]
    width = x.shape[-1]
    steps = count * slots // GROUP

    def at(m, s):
        group, slot, _ = place_of(steps - 1 - s, count)
        return (group, m, slot, 0, 0)

    def at_state(m, s):
        group, slot, _ = place_of(steps - 1 - s, count)
        return (group, m, slot, 0, 0, 0)

    def at_tail(m, s):
        step = jnp.maximum(steps - 2 - s, 0)
        group, slot, first = place_of(step, count)
        device = group * GROUP + jnp.where(first, GROUP - 1, 0)
        return (device, m, slot, C // PAD - 1, 0)

    def block(columns):
        return pl.BlockSpec((GROUP, 1, 1, C, columns), at)

    whole = lambda shape: pl.BlockSpec(shape, lambda m, s: (0,) * len(shape))
    rows = GROUP * C
    return pl.pallas_call(
        partial(backward_kernel, count, steps),
        grid=(micros, steps),
        in_specs=[
            pl.BlockSpec(memory_space=pltpu.SMEM),
            block(width),
            block(HEAD_SIZE),
            block(4 * HEAD_SIZE),
            pl.BlockSpec((1, 1, 1, PAD, 4 * HEAD_SIZE), at_tail),
            block(HEAD_SIZE),
            pl.BlockSpec((GROUP, 1, 1, 2, HEAD_SIZE, HEAD_SIZE), at_state),
            whole(taps.shape),
            whole(ridge.shape),
        ],
        out_specs=[
            block(4 * HEAD_SIZE),
            whole((4 * HEAD_SIZE, width)),
            whole((PAD, 3 * HEAD_SIZE)),
            whole((1, HEAD_SIZE)),
        ],
        out_shape=[
            jax.ShapeDtypeStruct((count, micros, slots, C, 4 * HEAD_SIZE), BF),
            jax.ShapeDtypeStruct((4 * HEAD_SIZE, width), F32),
            jax.ShapeDtypeStruct((PAD, 3 * HEAD_SIZE), F32),
            jax.ShapeDtypeStruct((1, HEAD_SIZE), F32),
        ],
        scratch_shapes=[
            pltpu.VMEM((rows + PAD, 3 * HEAD_SIZE), F32),
            pltpu.VMEM((rows, 3 * HEAD_SIZE), F32),
            pltpu.VMEM((rows, 3 * HEAD_SIZE), F32),
            pltpu.VMEM((rows, HEAD_SIZE), F32),
            pltpu.VMEM((rows, HEAD_SIZE), F32),
            pltpu.VMEM((rows, HEAD_SIZE), F32),
            pltpu.VMEM((rows, HEAD_SIZE), F32),
            pltpu.VMEM((rows, HEAD_SIZE), F32),
            pltpu.VMEM((rows + PAD, 3 * HEAD_SIZE), F32),
            pltpu.VMEM((HEAD_SIZE, HEAD_SIZE), F32),
            pltpu.VMEM((HEAD_SIZE, HEAD_SIZE), F32),
        ],
        compiler_params=pltpu.CompilerParams(vmem_limit_bytes=VMEM_BYTES),
        cost_estimate=pl.CostEstimate(
            flops=2 * count * micros * slots * C * (width * 512 + 24 * C * C),
            bytes_accessed=count * micros * slots * C * (2 * width + 4096),
            transcendentals=0,
        ),
        name="attn_backward",
    )(lengths, x, d_gated, pre, pre, mixed, states, taps, ridge)


def ff_kernel(
    x_ref, up_ref, mid_ref, wg_ref, wu_ref, wd_ref,
    res_ref, d2_ref, gg_ref, gu_ref, gd_ref, total,
):
    tile = pl.program_id(0)
    last = pl.num_programs(0) - 1

    @pl.when(tile == 0)
    def _():
        total[...] = mid_ref[...]
        d2_ref[...] = jnp.zeros_like(d2_ref)

    x = x_ref[...]
    up = up_ref[...]
    swish_pre = nn(x, wg_ref[...])
    lift = nn(x, wu_ref[...])
    sig = jax.nn.sigmoid(swish_pre)
    swish = swish_pre * sig
    hidden = (swish * lift).astype(BF)
    total[...] += nn(hidden, wd_ref[...])
    d_hidden = nt(up, wd_ref[...])
    d_swish = (d_hidden * lift * (sig * (1.0 + swish_pre * (1.0 - sig)))).astype(BF)
    d_lift = (d_hidden * swish).astype(BF)
    d2_ref[...] += nt(d_swish, wg_ref[...]) + nt(d_lift, wu_ref[...])
    gg_ref[...] = tn(d_swish, x).astype(BF)
    gu_ref[...] = tn(d_lift, x).astype(BF)
    gd_ref[...] = tn(up, hidden).astype(BF)

    @pl.when(tile == last)
    def _():
        res_ref[...] = total[...].astype(BF)


def feed_forward(x, up, middle, wg, wu, wd):
    rows, width = x.shape
    ff = wg.shape[1]
    tile = 256
    whole = pl.BlockSpec((rows, width), lambda t: (0, 0))
    across = pl.BlockSpec((width, tile), lambda t: (0, t))
    down = pl.BlockSpec((tile, width), lambda t: (t, 0))
    return pl.pallas_call(
        ff_kernel,
        grid=(ff // tile,),
        in_specs=[whole, whole, whole, across, across, down],
        out_specs=[whole, whole, down, down, across],
        out_shape=[
            jax.ShapeDtypeStruct((rows, width), BF),
            jax.ShapeDtypeStruct((rows, width), F32),
            jax.ShapeDtypeStruct((ff, width), BF),
            jax.ShapeDtypeStruct((ff, width), BF),
            jax.ShapeDtypeStruct((width, ff), BF),
        ],
        scratch_shapes=[pltpu.VMEM((rows, width), F32)],
        compiler_params=pltpu.CompilerParams(vmem_limit_bytes=VMEM_BYTES),
        cost_estimate=pl.CostEstimate(
            flops=18 * rows * width * ff, bytes_accessed=12 * width * ff, transcendentals=rows * ff
        ),
        name="feed_forward",
    )(x, up, middle, wg, wu, wd)


def body(
    tokens,
    lengths,
    w_query,
    w_key,
    w_value,
    w_mixgate,
    w_output,
    w_ffgate,
    w_ffup,
    w_ffdown,
    conv_weight,
    norm_first,
    norm_second,
    ridge_log,
    out_grad,
):
    micros, _, rows, width = tokens.shape
    taps_count = conv_weight.shape[1]
    count = lax.axis_size("ctx")
    shards = lax.axis_size("fsdp")
    place = lax.axis_index("ctx")
    share = count // HEAD_COUNT
    own = max(micros // share, 1)
    copies = share * own // micros
    head = place // share
    column = head * HEAD_SIZE
    slots = rows // C
    every = micros * rows
    both = ("ctx", "fsdp")

    def gathered(w):
        return lax.all_gather(w, "fsdp", axis=0, tiled=True)

    def of_head(w, axis):
        return lax.dynamic_slice_in_dim(w, column, HEAD_SIZE, axis)

    inputs = tokens.reshape(every, width).astype(F32)
    first_scale = lax.rsqrt(jnp.mean(inputs * inputs, -1, keepdims=True) + EPS)
    normed = (inputs * first_scale * norm_first).astype(BF)
    x = lax.all_gather(normed.reshape(micros, rows, width), "ctx", axis=0)
    mine = lax.rem(place, share) // copies * own
    if share > 1:
        x = lax.dynamic_slice_in_dim(x, mine, own, 1)
    x = x.reshape(count, own, slots, C, width)
    own_lengths = lax.dynamic_slice_in_dim(lengths[:, 0], mine, own, 0)
    projections = (w_query, w_key, w_value, w_mixgate)
    w_head = gathered(jnp.concatenate([of_head(w, 1) for w in projections], 1))
    taps = of_head(conv_weight, 2).transpose(1, 0, 2).reshape(taps_count, 3 * HEAD_SIZE)
    ridge = jnp.exp(of_head(ridge_log, 0))[None]
    gated_head, pre, mixed, states = attention_forward(own_lengths, x, w_head, taps, ridge)

    def to_rows(value):
        columns = value.shape[-1]
        value = lax.all_to_all(value.reshape(count, own, rows, columns), "ctx", 0, 0)
        value = value.reshape(HEAD_COUNT, share // copies, copies, own, rows, columns)[:, :, 0]
        value = value.reshape(HEAD_COUNT, micros, rows, columns)
        return value.transpose(1, 2, 0, 3).reshape(every, HEAD_COUNT, columns)

    def to_heads(value):
        value = value.reshape(micros, rows, HEAD_COUNT, HEAD_SIZE).transpose(2, 0, 1, 3)
        value = value.reshape(HEAD_COUNT, share // copies, 1, own, rows, HEAD_SIZE)
        value = jnp.broadcast_to(value, (*value.shape[:2], copies, *value.shape[3:]))
        value = lax.all_to_all(value.reshape(count, own, rows, HEAD_SIZE), "ctx", 0, 0)
        return value.reshape(count, own, slots, C, HEAD_SIZE)

    full_output = gathered(w_output)
    full_ffgate = gathered(w_ffgate)
    full_ffup = gathered(w_ffup)
    full_ffdown = gathered(w_ffdown)
    gated = to_rows(gated_head).reshape(every, width)
    middle = inputs + nn(gated, full_output)
    second_scale = lax.rsqrt(jnp.mean(middle * middle, -1, keepdims=True) + EPS)
    normed_two = (middle * second_scale * norm_second).astype(BF)
    upstream = out_grad.reshape(every, width)
    result, grad_two, gate_t, up_t, down_t = feed_forward(
        normed_two, upstream, middle, full_ffgate, full_ffup, full_ffdown
    )
    scaled_two = grad_two * norm_second
    gain_second = jnp.sum(grad_two * middle * second_scale, 0)
    grad_middle = (
        second_scale * scaled_two
        - middle * second_scale**3 * jnp.mean(scaled_two * middle, -1, keepdims=True)
        + upstream.astype(F32)
    )
    grad_branch = grad_middle.astype(BF)
    output_t = tn(grad_branch, gated).astype(BF)
    grad_gated = nt(grad_branch, full_output).astype(BF)
    d_pre, dw, dtaps, dridge = attention_backward(
        own_lengths, x, to_heads(grad_gated), pre, mixed, states, taps, ridge
    )

    def scattered(value):
        return lax.psum_scatter(value, both, scatter_dimension=0, tiled=True).astype(F32).T

    grad_ffgate = scattered(gate_t)
    grad_ffup = scattered(up_t)
    grad_ffdown = scattered(down_t)
    grad_output = scattered(output_t)

    piece = HEAD_SIZE // share // shards
    dw = dw.reshape(4, share, shards, piece, width).transpose(1, 2, 0, 3, 4).astype(BF)
    small = jnp.concatenate(
        [
            dtaps[:taps_count].reshape(taps_count, 3, HEAD_SIZE).transpose(1, 0, 2).reshape(3 * taps_count, HEAD_SIZE),
            dridge * ridge,
        ],
        0,
    )
    small = small.reshape(-1, share, shards, piece).transpose(1, 2, 0, 3)
    if share > 1:
        groups = [[h * share + i for i in range(share)] for h in range(HEAD_COUNT)]
        counts = lax.rem(place, copies) == 0
        dw = jnp.where(counts, dw, jnp.zeros_like(dw))
        small = jnp.where(counts, small, 0.0)
        dw = lax.psum_scatter(dw, "ctx", scatter_dimension=0, axis_index_groups=groups)
        small = lax.psum_scatter(small, "ctx", scatter_dimension=0, axis_index_groups=groups)
    else:
        dw = dw[0]
        small = small[0]
    dw = lax.psum_scatter(dw, "fsdp", scatter_dimension=0).astype(F32).transpose(0, 2, 1)
    small = lax.psum_scatter(small, "fsdp", scatter_dimension=0)

    full = jnp.stack([gathered(w) for w in projections], 1)
    full = full.reshape(width, 4, HEAD_COUNT, HEAD_SIZE).transpose(0, 2, 1, 3).reshape(width, -1)
    grad_normed = nt(to_rows(d_pre).reshape(every, -1), full)
    scaled_first = grad_normed * norm_first
    gain_first = jnp.sum(grad_normed * inputs * first_scale, 0)
    grad_inputs = (
        first_scale * scaled_first
        - inputs * first_scale**3 * jnp.mean(scaled_first * inputs, -1, keepdims=True)
        + grad_middle
    )
    gains = jnp.stack([gain_first, gain_second], 0)
    gains = lax.psum_scatter(gains, both, scatter_dimension=1, tiled=True)
    conv_shard = small[: 3 * taps_count].reshape(3, taps_count, -1)
    return (
        result.reshape(tokens.shape),
        grad_inputs.astype(BF).reshape(tokens.shape),
        dw[0],
        dw[1],
        dw[2],
        dw[3],
        grad_output,
        grad_ffgate,
        grad_ffup,
        grad_ffdown,
        conv_shard,
        gains[0],
        gains[1],
        small[3 * taps_count],
    )


def solution(mesh):
    rows = P(None, "fsdp", "ctx", None)
    weight = P("fsdp", None)
    grad = P(None, ("ctx", "fsdp"))
    line = P(("ctx", "fsdp"))
    return jax.shard_map(
        body,
        mesh=mesh,
        in_specs=(rows, P(None, "fsdp"), *([weight] * 8), P(), P(), P(), P(), rows),
        out_specs=(rows, rows, *([grad] * 8), P(None, None, ("ctx", "fsdp")), line, line, line),
        check_vma=False,
    )
```

time: 2960 us -> 1210 us (0.41)
  waiting for transfers between devices: 2230 us -> 935 us
  matrix products: 331 us -> 14.5 us
  Pallas kernels: 0 us -> 146 us
  local copies, waits for them, and re-layouts: 180 us -> 41.2 us
  other arithmetic: 141 us -> 29 us
    unnamed x80 -> x17, waiting for transfers between devices: 1180 us -> 136 us
    dot_general x112 -> x4, matrix products: 331 us -> 14.5 us  [the longest x2 7.4 us: nt(): lax.dot_general(a, b, (((1,), (1,)), ((), ())), preferred_element_type=F32)]
    all_gather x16 -> x10, waiting for transfers between devices: 506 us -> 220 us  [the longest x1 128 us: body(): x = lax.all_gather(normed.reshape(micros, rows, width), 'ctx', axis=0)]
    pallas_call x0 -> x3, Pallas kernels: none -> 146 us  [the longest x1 65.1 us: attention_backward(): pl.pallas_call(partial(backward_kernel, count, steps), grid=(micros, step...]
    all_to_all x0 -> x3, waiting for transfers between devices: none -> 116 us  [the longest x2 90.5 us: to_rows(): lax.all_to_all(value.reshape(count, own, rows, columns), 'ctx', 0, 0)]
    unnamed x444 -> x37, local copies, waits for them, and re-layouts: 114 us -> 7.05 us
    reduce_scatter x8 -> x5, waiting for transfers between devices: 546 us -> 463 us  [the longest x4 463 us: scattered(): lax.psum_scatter(value, both, scatter_dimension=0, tiled=True).astype(F32)]
    select_n x17 -> x0, other arithmetic: 40 us -> none  [the longest x16 40 us: hop(): return jnp.where(reached, new, before)]
  transfers between devices with their start and end apart: 60 -> 19, of which waited for: 48 -> 12; matrix products, arithmetic and copies ran while one was open for 17% -> 6% of each run, Pallas kernels for 0% -> 12%
where the time goes in v1:
time: 1210 us
  waiting for transfers between devices  935 us (77%)
  Pallas kernels  146 us (12%)
  local copies, waits for them, and re-layouts  41.2 us (3%)
  other arithmetic  29 us (2%)
  starting transfers between devices  15 us (1%)
  matrix products  14.5 us (1%)
  between operations  14.2 us (1%)
    reduce_scatter x4, waiting for transfers between devices, scattered(): lax.psum_scatter(value, both, scatter_dimension=0, tiled=True).astype(F32)  463 us
    unnamed x17, waiting for transfers between devices  136 us
    all_gather x1, waiting for transfers between devices, body(): x = lax.all_gather(normed.reshape(micros, rows, width), 'ctx', axis=0)  128 us
    all_gather x9, waiting for transfers between devices, gathered(): return lax.all_gather(w, 'fsdp', axis=0, tiled=True)  92.4 us
    all_to_all x2, waiting for transfers between devices, to_rows(): lax.all_to_all(value.reshape(count, own, rows, columns), 'ctx', 0, 0)  90.5 us
    pallas_call x1, Pallas kernels, attention_backward(): pl.pallas_call(partial(backward_kernel, count, steps), grid=(micros, step...  65.1 us
    pallas_call x1, Pallas kernels, feed_forward(): pl.pallas_call(ff_kernel, grid=(ff // tile,), in_specs=[whole, whole, who...  41.2 us
    pallas_call x1, Pallas kernels, attention_forward(): pl.pallas_call(partial(forward_kernel, count), grid=(micros, steps), in_s...  40 us
  transfers between devices with their start and end apart: 19, of which 12 were waited for; matrix products, arithmetic and copies ran while one was open for 6% of the time, Pallas kernels for 12%

profile of v1, /device:TPU:0, one launch (start us, length us, event | category | flops | bytes accessed | tf_op | source)
XLA Modules:
  0.0 1205.7 jit_solution(12553356198213683378)
XLA Ops:
  20.2 10.8 all-gather.13.cloned.1.call-done.w_ref
  31.1 127.7 %all-gather.11.cloned.1.call-done = bf16[8,2,256,1024]{3,2,1,0:T(8,128)(2,1)} async-done(((bf16[1,2,256,1024]{3,2,1,0:T(8,128)(2,1)}), bf16[8,2,256,1024]{3,2,1,0:T(8,128)(2,1)}) %all-gather.11.cloned.1.call-update) | async-done | bytes 8388624 | tf_op jit(solution)/shard_map/all_gather | solution.py:510
  158.7 40.0 %attn_forward.1 = (bf16[8,2,2,128,128]{4,3,2,1,0:T(8,128)(2,1)}, f32[8,2,2,128,512]{4,3,2,1,0:T(8,128)}, f32[8,2,2,128,128]{4,3,2,1,0:T(8,128)}, f32[8,2,2,2,128,128]{5,4,3,2,1,0:T(8,128)}) custom-call(s32[2]{0:T(128)} %bitcast.167, bf16[8,2,2,128,1024]{4,3,2,1,0:T(8,128)(2,1)} %bitcast.138, bf16[1024,512]{1,0:T(8,128)(2,1)} %all-gather.13.cloned.1.call-done.w_ref, ...), custom_call_target="tpu_custom_call" | custom-call | flops 5771362304 | bytes 25165824 | tf_op jit(solution)/shard_map/attn_forward/pallas_call | solution.py:163
  203.0 24.9 %all-to-all-done = bf16[8,2,256,128]{3,2,1,0:T(8,128)(2,1)S(1)} async-done(((bf16[8,2,256,128]{3,2,1,0:T(8,128)(2,1)}), bf16[8,2,256,128]{3,2,1,0:T(8,128)(2,1)S(1)}, u32[]{:S(2)}, u32[]{:S(2)}) %all-to-all-start) | async-done | bytes 1048608 | tf_op jit(solution)/shard_map/all_to_all | solution.py:524
  234.3 36.7 %all-gather.19.cloned.1.call-done.wu_ref = bf16[1024,2816]{1,0:T(8,128)(2,1)} async-done(((bf16[256,2816]{1,0:T(8,128)(2,1)}), bf16[1024,2816]{1,0:T(8,128)(2,1)}) %all-gather.19.cloned.1.call-update) | async-done | bytes 5767184 | tf_op jit(solution)/shard_map/all_gather | solution.py:502
  271.0 44.9 %all-gather.21.cloned.1.call-done.wd_ref = bf16[2816,1024]{1,0:T(8,128)(2,1)} async-done(((bf16[704,1024]{1,0:T(8,128)(2,1)}), bf16[2816,1024]{1,0:T(8,128)(2,1)}) %all-gather.21.cloned.1.call-update) | async-done | bytes 5767184 | tf_op jit(solution)/shard_map/all_gather | solution.py:502
  315.8 41.2 %feed_forward.1 = (bf16[512,1024]{1,0:T(8,128)(2,1)}, f32[512,1024]{1,0:T(8,128)}, bf16[2816,1024]{1,0:T(8,128)(2,1)}, bf16[2816,1024]{1,0:T(8,128)(2,1)}, bf16[1024,2816]{1,0:T(8,128)(2,1)}) custom-call(bf16[512,1024]{1,0:T(8,128)(2,1)} %multiply_convert_fusion.x_ref, bf16[512,1024]{1,0:T(8,128)(2,1)} %bitcast.152, f32[512,1024]{1,0:T(8,128)} %copy-done.2, ...), custom_call_target="tpu_custom_call" | custom-call | flops 26575110144 | bytes 34603008 | tf_op jit(solution)/shard_map/feed_forward/pallas_call | solution.py:449
  364.9 5.5 all-to-all-start.1
  371.0 25.7 %all-to-all-done.1 = bf16[8,2,256,128]{3,2,1,0:T(8,128)(2,1)} async-done(((bf16[8,2,256,128]{3,2,1,0:T(8,128)(2,1)}), bf16[8,2,256,128]{3,2,1,0:T(8,128)(2,1)}, u32[]{:S(2)}, u32[]{:S(2)}) %all-to-all-start.1) | async-done | bytes 1048608 | tf_op jit(solution)/shard_map/all_to_all | solution.py:533
  396.7 65.1 %attn_backward.1 = (bf16[8,2,2,128,512]{4,3,2,1,0:T(8,128)(2,1)}, f32[512,1024]{1,0:T(8,128)}, f32[8,384]{1,0:T(8,128)}, f32[1,128]{1,0:T(1,128)}) custom-call(s32[2]{0:T(128)} %bitcast.168, bf16[8,2,2,128,1024]{4,3,2,1,0:T(8,128)(2,1)} %bitcast.139, bf16[8,2,2,128,128]{4,3,2,1,0:T(8,128)(2,1)} %bitcast.14.g_ref, ...), custom_call_target="tpu_custom_call" | custom-call | flops 7516192768 | bytes 25165824 | tf_op jit(solution)/shard_map/attn_backward/pallas_call | solution.py:360
  461.8 4.6 all-to-all-start.2
  473.6 4.0 copy.49
  477.6 4.0 copy.50
  485.5 4.0 copy.52
  489.6 7.2 pad_maximum_fusion
  496.8 65.7 %all-to-all-done.2 = bf16[8,2,256,512]{3,2,1,0:T(8,128)(2,1)} async-done(((bf16[8,2,256,512]{3,2,1,0:T(8,128)(2,1)}), bf16[8,2,256,512]{3,2,1,0:T(8,128)(2,1)}, u32[]{:S(2)}, u32[]{:S(2)}) %all-to-all-start.2) | async-done | bytes 4194336 | tf_op jit(solution)/shard_map/all_to_all | solution.py:524
  562.4 4.7 copy.48
  569.5 6.1 fusion.9
  580.1 10.3 all-reduce
  594.6 42.2 %reduce-scatter.12.cloned.1.call-done = bf16[32,1024]{1,0:T(8,128)(2,1)} async-done(((bf16[1024,1024]{1,0:T(8,128)(2,1)}), bf16[32,1024]{1,0:T(8,128)(2,1)}) %reduce-scatter.12.cloned.1.call-update) | async-done | bytes 65552 | tf_op jit(solution)/shard_map/reduce_scatter | solution.py:563
  641.5 129.8 %reduce-scatter.20.cloned.1.call-done = f32[32,2]{1,0:T(8,128)} async-done(((f32[1024,2]{1,0:T(8,128)}), f32[32,2]{1,0:T(8,128)}) %reduce-scatter.20.cloned.1.call-update) | async-done | bytes 272
  773.3 140.0 %reduce-scatter.16.cloned.1.call-done = bf16[88,1024]{1,0:T(8,128)(2,1)} async-done(((bf16[2816,1024]{1,0:T(8,128)(2,1)}), bf16[88,1024]{1,0:T(8,128)(2,1)}) %reduce-scatter.16.cloned.1.call-update) | async-done | bytes 180240 | tf_op jit(solution)/shard_map/reduce_scatter | solution.py:563
  915.0 140.5 %reduce-scatter.18.cloned.1.call-done = bf16[32,2816]{1,0:T(8,128)(2,1)} async-done(((bf16[1024,2816]{1,0:T(8,128)(2,1)}), bf16[32,2816]{1,0:T(8,128)(2,1)}) %reduce-scatter.18.cloned.1.call-update) | async-done | bytes 180240 | tf_op jit(solution)/shard_map/reduce_scatter | solution.py:563
  1057.2 140.3 %reduce-scatter.14.cloned.1.call-done = bf16[88,1024]{1,0:T(8,128)(2,1)} async-done(((bf16[2816,1024]{1,0:T(8,128)(2,1)}), bf16[88,1024]{1,0:T(8,128)(2,1)}) %reduce-scatter.14.cloned.1.call-update) | async-done | bytes 180240 | tf_op jit(solution)/shard_map/reduce_scatter | solution.py:563
  (118 shorter events, 65.7 us)
Async XLA Ops:
  7.2 12.5 %copy-start = (f32[3,4,1024]{2,1,0:T(4,128)S(1)}, f32[3,4,1024]{2,1,0:T(4,128)}, u32[]{:S(2)}) copy-start(f32[3,4,1024]{2,1,0:T(4,128)} %param.25) | copy-start | bytes 147460
  7.2 23.9 %all-gather.13.cloned.1.call-start = ((), (), s32[]{:S(2)}) async-start(), calls=%async_computation.10 | async-start | bytes 1310720 | tf_op jit(solution)/shard_map/all_gather | solution.py:502
  11.5 147.2 %all-gather.11.cloned.1.call-start = ((), (), s32[]{:S(2)}) async-start(), calls=%async_computation.9 | async-start | bytes 9437184 | tf_op jit(solution)/shard_map/all_gather | solution.py:510
  14.4 215.1 %all-gather.15.cloned.1.call-start = ((), (), s32[]{:S(2)}) async-start(), calls=%async_computation.11 | async-start | bytes 2621440 | tf_op jit(solution)/shard_map/all_gather | solution.py:502
  15.1 219.2 %all-gather.17.cloned.1.call-start = ((), (), s32[]{:S(2)}) async-start(), calls=%async_computation.12 | async-start | bytes 7208960 | tf_op jit(solution)/shard_map/all_gather | solution.py:502
  15.7 255.3 %all-gather.19.cloned.1.call-start = ((), (), s32[]{:S(2)}) async-start(), calls=%async_computation.13 | async-start | bytes 7208960 | tf_op jit(solution)/shard_map/all_gather | solution.py:502
  16.3 299.5 %all-gather.21.cloned.1.call-start = ((), (), s32[]{:S(2)}) async-start(), calls=%async_computation.14 | async-start | bytes 7208960 | tf_op jit(solution)/shard_map/all_gather | solution.py:502
  16.9 456.8 %all-gather.23.cloned.1.call-start = ((), (), s32[]{:S(2)}) async-start(), calls=%async_computation.15 | async-start | bytes 2621440 | tf_op jit(solution)/shard_map/all_gather | solution.py:502
  17.6 460.0 %all-gather.25.cloned.1.call-start = ((), (), s32[]{:S(2)}) async-start(), calls=%async_computation.16 | async-start | bytes 2621440 | tf_op jit(solution)/shard_map/all_gather | solution.py:502
  198.7 29.2 %all-to-all-start = ((bf16[8,2,256,128]{3,2,1,0:T(8,128)(2,1)}), bf16[8,2,256,128]{3,2,1,0:T(8,128)(2,1)S(1)}, u32[]{:S(2)}, u32[]{:S(2)}) async-start(bf16[8,2,256,128]{3,2,1,0:T(8,128)(2,1)} %bitcast.155), calls=%async_computation | async-start | bytes 2097152 | tf_op jit(solution)/shard_map/all_to_all | solution.py:524
  202.3 279.3 %all-gather.27.cloned.1.call-start = ((), (), s32[]{:S(2)}) async-start(), calls=%async_computation.17 | async-start | bytes 2621440 | tf_op jit(solution)/shard_map/all_gather | solution.py:502
  232.8 83.0 %copy-start.2 = (f32[512,1024]{1,0:T(8,128)}, f32[512,1024]{1,0:T(8,128)S(1)}, u32[]{:S(2)}) copy-start(f32[512,1024]{1,0:T(8,128)S(1)} %get-tuple-element.97.mid_ref) | copy-start | bytes 6291460
  315.8 44.2 %copy-start.6 = (bf16[2,1,256,1024]{3,2,1,0:T(8,128)(2,1)S(1)}, bf16[2,1,256,1024]{3,2,1,0:T(8,128)(2,1)}, u32[]{:S(2)}) copy-start(bf16[2,1,256,1024]{3,2,1,0:T(8,128)(2,1)} %param.29) | copy-start | bytes 3145732
  364.9 31.8 %all-to-all-start.1 = ((bf16[8,2,256,128]{3,2,1,0:T(8,128)(2,1)}), bf16[8,2,256,128]{3,2,1,0:T(8,128)(2,1)}, u32[]{:S(2)}, u32[]{:S(2)}) async-start(bf16[8,2,256,128]{3,2,1,0:T(8,128)(2,1)} %bitcast.149), calls=%async_computation.1 | async-start | bytes 2097152 | tf_op jit(solution)/shard_map/all_to_all | solution.py:533
  370.4 115.1 %all-gather.29.cloned.1.call-start = ((), (), s32[]{:S(2)}) async-start(), calls=%async_computation.18 | async-start | bytes 2621440 | tf_op jit(solution)/shard_map/all_gather | solution.py:502
  461.8 100.6 %all-to-all-start.2 = ((bf16[8,2,256,512]{3,2,1,0:T(8,128)(2,1)}), bf16[8,2,256,512]{3,2,1,0:T(8,128)(2,1)}, u32[]{:S(2)}, u32[]{:S(2)}) async-start(bf16[8,2,256,512]{3,2,1,0:T(8,128)(2,1)} %bitcast.145), calls=%async_computation.2 | async-start | bytes 8388608 | tf_op jit(solution)/shard_map/all_to_all | solution.py:524
  466.5 126.4 %reduce-scatter.10.cloned.1.call-start = ((), (), s32[]{:S(2)}) async-start(), calls=%async_computation.19 | async-start | bytes 1310720 | tf_op jit(solution)/shard_map/reduce_scatter | solution.py:590
  469.4 167.5 %reduce-scatter.12.cloned.1.call-start = ((), (), s32[]{:S(2)}) async-start(), calls=%async_computation.20 | async-start | bytes 2162688 | tf_op jit(solution)/shard_map/reduce_scatter | solution.py:563
  473.3 298.0 %reduce-scatter.20.cloned.1.call-start = ((), (), s32[]{:S(2)}) async-start(), calls=%async_computation.24 | async-start | bytes 540672
  562.4 7.0 slice-start
  576.7 336.6 %reduce-scatter.16.cloned.1.call-start = ((), (), s32[]{:S(2)}) async-start(), calls=%async_computation.22 | async-start | bytes 5947392 | tf_op jit(solution)/shard_map/reduce_scatter | solution.py:563
  577.3 478.2 %reduce-scatter.18.cloned.1.call-start = ((), (), s32[]{:S(2)}) async-start(), calls=%async_computation.23 | async-start | bytes 5947392 | tf_op jit(solution)/shard_map/reduce_scatter | solution.py:563
  577.9 619.7 %reduce-scatter.14.cloned.1.call-start = ((), (), s32[]{:S(2)}) async-start(), calls=%async_computation.21 | async-start | bytes 5947392 | tf_op jit(solution)/shard_map/reduce_scatter | solution.py:563
  638.3 560.9 %copy-start.1 = (f32[3,4,1024]{2,1,0:T(4,128)S(1)}, f32[3,4,1024]{2,1,0:T(4,128)}, u32[]{:S(2)}) copy-start(f32[3,4,1024]{2,1,0:T(4,128)} %param.25) | copy-start | bytes 147460
  (10 other events, 28.7 us)
Sparse Core Ops, SparseCore 0:
  11.6 19.4 all-gather.12
  33.8 124.9 all-gather.10
  160.3 20.8 all-gather.14
  182.6 43.4 all-gather.16
  227.5 43.4 all-gather.18
  272.4 43.3 all-gather.20
  317.4 22.5 all-gather.22
  341.6 22.5 all-gather.24
  365.7 22.5 all-gather.26
  389.8 22.6 all-gather.28
  469.8 25.2 reduce-scatter.9
  497.3 139.4 reduce-scatter.11
  639.0 132.1 reduce-scatter.19
  773.5 139.7 reduce-scatter.15
  915.6 139.8 reduce-scatter.17
  1057.7 139.7 reduce-scatter.13

commit v2 on v1

--- a/solution.py
+++ b/solution.py
@@ -63,25 +63,51 @@
     return (pos < length).astype(F32)
 
 
-def solve(q, k, kb, skk, ridge, tri):
-    system = jnp.concatenate([kb, skk], 0)
-    qb = q.astype(BF)
-    inner0 = jnp.where(tri, nt(qb, kb), 0.0)
-    i0 = nn(jnp.concatenate([inner0.astype(BF), qb], 1), system) + ridge * q
-    rr0 = rowsum(q * q)
-    p0 = rowsum(q * i0)
-    a0 = rr0 / p0
-    r1 = q - a0 * i0
-    f = rowsum(r1 * r1)
-    b = f / rr0
-    d1 = r1 + b * q
-    db = d1.astype(BF)
-    inner1 = jnp.where(tri, nt(db, kb), 0.0)
-    i1 = nn(jnp.concatenate([inner1.astype(BF), db], 1), system) + ridge * d1
-    p1 = rowsum(d1 * i1)
-    a1 = f / p1
-    s2 = a0 * q + a1 * d1
-    return system, qb, inner0, i0, rr0, p0, a0, r1, f, b, d1, inner1, i1, p1, a1, s2
+def split(v):
+    high = v.astype(BF)
+    return high, (v - high.astype(F32)).astype(BF)
+
+
+def fine(product, a, b):
+    (ah, al), (bh, bl) = a, b
+    return product(ah, bh) + (product(ah, bl) + product(al, bh))
+
+
+def each(f, *lists):
+    return [f(*values) for values in zip(*lists)]
+
+
+def masked(tri, values):
+    return [jnp.where(tri, v, 0.0) for v in values]
+
+
+def low(values):
+    return [v.astype(BF) for v in values]
+
+
+def beside(a, b):
+    return jnp.concatenate([a, b], 1)
+
+
+def solve(q, kb, skk, ridge, tri):
+    system = each(lambda k, s: jnp.concatenate([k, s], 0), kb, skk)
+    qb = low(q)
+    inner0 = masked(tri, each(nt, qb, kb))
+    i0 = each(lambda n, d, m, v: nn(beside(n, d), m) + ridge * v, low(inner0), qb, system, q)
+    rr0 = each(lambda v: rowsum(v * v), q)
+    p0 = each(lambda v, i: rowsum(v * i), q, i0)
+    a0 = each(lambda r, p: r / p, rr0, p0)
+    r1 = each(lambda v, a, i: v - a * i, q, a0, i0)
+    f = each(lambda v: rowsum(v * v), r1)
+    b = each(lambda v, r: v / r, f, rr0)
+    d1 = each(lambda r, w, v: r + w * v, r1, b, q)
+    db = low(d1)
+    inner1 = masked(tri, each(nt, db, kb))
+    i1 = each(lambda n, d, m, v: nn(beside(n, d), m) + ridge * v, low(inner1), db, system, d1)
+    p1 = each(lambda v, i: rowsum(v * i), d1, i1)
+    a1 = each(lambda v, p: v / p, f, p1)
+    s2 = each(lambda a, v, w, d: a * v + w * d, a0, q, a1, d1)
+    return system, qb, inner0, i0, rr0, p0, a0, r1, f, b, d1, db, inner1, i1, p1, a1, s2
 
 
 def forward_kernel(
@@ -117,29 +143,33 @@
     v_s[...] = act[:, 2 * HEAD_SIZE :] * valid
     tri = causal_mask()
     ridge = ridge_ref[...]
+    places = [jnp.where(first, j, GROUP - 1 - j) for j in range(GROUP)]
+    rows = [slice(j * C, (j + 1) * C) for j in range(GROUP)]
+    keys = [split(k_s[r, :]) for r in rows]
+    values = [split(v_s[r, :]) for r in rows]
+    kb = [k[0] for k in keys]
+    kk_all, kv_all = [skk[...]], [skv[...]]
     for j in range(GROUP):
-        jj = jnp.where(first, j, GROUP - 1 - j)
-        rows = slice(j * C, (j + 1) * C)
-        k = k_s[rows, :]
-        kb = k.astype(BF)
-        vb = v_s[rows, :].astype(BF)
-        kk_now = skk[...]
-        kv_now = skv[...]
-        states_ref[jj, 0, 0, 0] = kk_now
-        states_ref[jj, 0, 0, 1] = kv_now
-        s2 = solve(q_s[rows, :], k, kb, kk_now.astype(BF), ridge, tri)[-1]
-        sb = s2.astype(BF)
-        p = jnp.where(tri, nt(sb, kb), 0.0)
-        mixed = nn(
-            jnp.concatenate([p.astype(BF), sb], 1),
-            jnp.concatenate([vb, kv_now.astype(BF)], 0),
-        )
-        mixed = mixed * valid[rows, :]
-        mixed_ref[jj, 0, 0] = mixed
+        kk_all.append(kk_all[j] + tn(kb[j], kb[j]))
+        kv_all.append(kv_all[j] + fine(tn, keys[j], values[j]))
+    skk[...] = kk_all[GROUP]
+    skv[...] = kv_all[GROUP]
+    for j, jj in enumerate(places):
+        states_ref[jj, 0, 0, 0] = kk_all[j]
+        states_ref[jj, 0, 0, 1] = kv_all[j]
+    queries = [q_s[r, :] for r in rows]
+    s2 = solve(queries, kb, low(kk_all[:GROUP]), ridge, tri)[-1]
+    parts = [split(v) for v in s2]
+    weights = [split(jnp.where(tri, fine(nt, a, k), 0.0)) for a, k in zip(parts, keys)]
+    states = [split(v) for v in kv_all[:GROUP]]
+    mixed = [
+        (fine(nn, w, v) + fine(nn, a, t)) * valid[r, :]
+        for w, v, a, t, r in zip(weights, values, parts, states, rows)
+    ]
+    for jj, v in zip(places, mixed):
+        mixed_ref[jj, 0, 0] = v
         gate = pre_ref[jj, 0, 0, :, 3 * HEAD_SIZE :]
-        gated_ref[jj, 0, 0] = (mixed * silu(gate)).astype(BF)
-        skk[...] = kk_now + tn(kb, kb)
-        skv[...] = kv_now + tn(kb, vb)
+        gated_ref[jj, 0, 0] = (v * silu(gate)).astype(BF)
 
 
 def attention_forward(lengths, x, w, taps, ridge):
@@ -242,69 +272,81 @@
     k_s[...] = act_k * (scale_k * valid)
     tri = causal_mask()
     ridge = ridge_ref[...]
-    ridge_total = jnp.zeros((1, HEAD_SIZE), F32)
-    for j in reversed(range(GROUP)):
-        jj = jnp.where(first, j, GROUP - 1 - j)
-        rows = slice(j * C, (j + 1) * C)
-        q = q_s[rows, :]
-        k = k_s[rows, :]
-        kb = k.astype(BF)
-        vb = (act_s[rows, 2 * HEAD_SIZE :] * valid[rows, :]).astype(BF)
-        skk = states_ref[jj, 0, 0, 0].astype(BF)
-        skv = states_ref[jj, 0, 0, 1].astype(BF)
-        system, qb, inner0, i0, rr0, p0, a0, r1, f, b, d1, inner1, i1, p1, a1, s2 = solve(
-            q, k, kb, skk, ridge, tri
-        )
+    places = [jnp.where(first, j, GROUP - 1 - j) for j in range(GROUP)]
+    rows = [slice(j * C, (j + 1) * C) for j in range(GROUP)]
+    q = [q_s[r, :] for r in rows]
+    keys = [split(k_s[r, :]) for r in rows]
+    kb = [k[0] for k in keys]
+    values = [split(act_s[r, 2 * HEAD_SIZE :] * valid[r, :]) for r in rows]
+    vb = [v[0] for v in values]
+    skk = [states_ref[jj, 0, 0, 0].astype(BF) for jj in places]
+    skv = [split(states_ref[jj, 0, 0, 1]) for jj in places]
+    g = []
+    for jj, r in zip(places, rows):
         gate = pre_ref[jj, 0, 0, :, 3 * HEAD_SIZE :]
         d_gated = g_ref[jj, 0, 0].astype(F32)
         dpre_ref[jj, 0, 0, :, 3 * HEAD_SIZE :] = (
             d_gated * mixed_ref[jj, 0, 0] * slope(gate)
         ).astype(BF)
-        g = (d_gated * silu(gate) * valid[rows, :]).astype(BF)
-        sb = s2.astype(BF)
-        p = jnp.where(tri, nt(sb, kb), 0.0)
-        back = jnp.where(tri, nt(g, vb), 0.0)
-        backb = back.astype(BF)
-        ds = nn(backb, kb) + nt(g, skv)
-        da1 = rowsum(ds * d1)
-        df = da1 / p1
-        dp1 = -df * a1
-        dd1 = a1 * ds + (2.0 * dp1) * i1
-        dbeta = rowsum(dd1 * q)
-        inv_rr = 1.0 / rr0
-        df = df + dbeta * inv_rr
-        drr = -dbeta * b * inv_rr
-        dr1 = dd1 + (2.0 * df) * r1
-        da0 = rowsum(ds * q - dr1 * i0)
-        da0p = da0 / p0
-        drr = drr + da0p
-        dp0 = -da0p * a0
-        drb = dr1.astype(BF)
-        innerr = jnp.where(tri, nt(drb, kb), 0.0)
-        adr = nn(jnp.concatenate([innerr.astype(BF), drb], 1), system) + ridge * dr1
-        dd0 = b * dd1 + a0 * ds + (2.0 * dp0) * i0 - a0 * adr
-        di0 = dp0 * q - a0 * dr1
-        dq_s[rows, :] = dr1 + dd0 + (2.0 * drr) * q
-        wd1 = (2.0 * dp1) * d1
-        ridge_total = ridge_total + jnp.sum(0.5 * wd1 * d1 + di0 * q, 0, keepdims=True)
-        inneri = dp0 * inner0 - a0 * innerr
-        di0b = di0.astype(BF)
-        d1b = d1.astype(BF)
-        wd1b = wd1.astype(BF)
-        left = jnp.concatenate(
-            [backb, inner1.astype(BF), inner0.astype(BF), inneri.astype(BF)], 0
-        )
-        right = jnp.concatenate([sb, wd1b, di0b, qb], 0)
-        g_now = gsum[...]
-        h_now = hsum[...]
-        hb = h_now.astype(BF)
-        dk_s[rows, :] = tn(left, right) + nn(kb, g_now.astype(BF)) + nt(vb, hb)
-        both = tn(jnp.concatenate([p.astype(BF), sb], 1), g)
-        dv_s[rows, :] = both[:C] + nn(kb, hb)
-        hsum[...] = h_now + both[C:]
-        gsum[...] = g_now + tn(
-            jnp.concatenate([d1b, di0b, qb], 0), jnp.concatenate([wd1b, qb, di0b], 0)
-        )
+        g.append(split(d_gated * silu(gate) * valid[r, :]))
+    gb = [v[0] for v in g]
+    system, qb, inner0, i0, rr0, p0, a0, r1, f, b, d1, d1b, inner1, i1, p1, a1, s2 = solve(
+        q, kb, skk, ridge, tri
+    )
+    back = masked(tri, [fine(nt, v, w) for v, w in zip(g, values)])
+    ds = [
+        fine(nn, split(w), k) + fine(nt, v, t) for w, k, v, t in zip(back, keys, g, skv)
+    ]
+    sb = low(s2)
+    p = low(masked(tri, each(nt, sb, kb)))
+    da1 = each(lambda v, d: rowsum(v * d), ds, d1)
+    df = each(lambda v, w: v / w, da1, p1)
+    dp1 = each(lambda v, a: -v * a, df, a1)
+    dd1 = each(lambda a, v, w, i: a * v + (2.0 * w) * i, a1, ds, dp1, i1)
+    dbeta = each(lambda v, w: rowsum(v * w), dd1, q)
+    inv_rr = each(lambda v: 1.0 / v, rr0)
+    df = each(lambda v, w, i: v + w * i, df, dbeta, inv_rr)
+    dr1 = each(lambda v, w, r: v + (2.0 * w) * r, dd1, df, r1)
+    drb = low(dr1)
+    innerr = masked(tri, each(nt, drb, kb))
+    adr = each(lambda n, d, m, v: nn(beside(n, d), m) + ridge * v, low(innerr), drb, system, dr1)
+    da0p = each(lambda v, w, r, i, z: rowsum(v * w - r * i) / z, ds, q, dr1, i0, p0)
+    drr = each(lambda v, w, i, z: z - v * w * i, dbeta, b, inv_rr, da0p)
+    dp0 = each(lambda v, a: -v * a, da0p, a0)
+    dd0 = each(
+        lambda w, v, a, t, e, i, m: w * v + a * t + (2.0 * e) * i - a * m,
+        b, dd1, a0, ds, dp0, i0, adr,
+    )
+    di0 = each(lambda e, v, a, r: e * v - a * r, dp0, q, a0, dr1)
+    for r, v, w, z, t in zip(rows, dr1, dd0, drr, q):
+        dq_s[r, :] = v + w + (2.0 * z) * t
+    wd1 = each(lambda e, d: (2.0 * e) * d, dp1, d1)
+    inneri = low(each(lambda e, n, a, m: e * n - a * m, dp0, inner0, a0, innerr))
+    di0b = low(di0)
+    wd1b = low(wd1)
+    ridge_total = sum(
+        jnp.sum(0.5 * w * d + e * v, 0, keepdims=True) for w, d, e, v in zip(wd1, d1, di0, q)
+    )
+    left = each(
+        lambda *parts: jnp.concatenate(parts, 0), low(back), low(inner1), low(inner0), inneri
+    )
+    right = each(lambda *parts: jnp.concatenate(parts, 0), sb, wd1b, di0b, qb)
+    near = each(tn, left, right)
+    both = each(lambda w, v, t: tn(beside(w, v), t), p, sb, gb)
+    outer = each(
+        lambda d, e, v, w: tn(jnp.concatenate([d, e, v], 0), jnp.concatenate([w, v, e], 0)),
+        d1b, di0b, qb, wd1b,
+    )
+    g_all, h_all = [gsum[...]], [hsum[...]]
+    for j in reversed(range(GROUP)):
+        g_all.insert(0, g_all[0] + outer[j])
+        h_all.insert(0, h_all[0] + both[j][C:])
+    gsum[...] = g_all[0]
+    hsum[...] = h_all[0]
+    for j, r in enumerate(rows):
+        hb = h_all[j + 1].astype(BF)
+        dk_s[r, :] = near[j] + nn(kb[j], g_all[j + 1].astype(BF)) + nt(vb[j], hb)
+        dv_s[r, :] = both[j][:C] + nn(kb[j], hb)
     dridge_ref[...] += ridge_total
     act = act_s[...]
     act_q = act[:, :HEAD_SIZE]
@@ -407,11 +449,12 @@
 
 
 def ff_kernel(
-    x_ref, up_ref, mid_ref, wg_ref, wu_ref, wd_ref,
-    res_ref, d2_ref, gg_ref, gu_ref, gd_ref, total,
+    x_ref, up_ref, mid_ref, xs_ref, us_ref, wg_ref, wu_ref, wd_ref,
+    res_ref, d2_ref, gk_ref, gs_ref, uk_ref, us_out_ref, dk_ref, ds_ref, total,
 ):
     tile = pl.program_id(0)
     last = pl.num_programs(0) - 1
+    half = xs_ref.shape[1] // 2
 
     @pl.when(tile == 0)
     def _():
@@ -419,44 +462,54 @@
         d2_ref[...] = jnp.zeros_like(d2_ref)
 
     x = x_ref[...]
-    up = up_ref[...]
     swish_pre = nn(x, wg_ref[...])
     lift = nn(x, wu_ref[...])
     sig = jax.nn.sigmoid(swish_pre)
     swish = swish_pre * sig
     hidden = (swish * lift).astype(BF)
     total[...] += nn(hidden, wd_ref[...])
-    d_hidden = nt(up, wd_ref[...])
+    d_hidden = nt(up_ref[...], wd_ref[...])
     d_swish = (d_hidden * lift * (sig * (1.0 + swish_pre * (1.0 - sig)))).astype(BF)
     d_lift = (d_hidden * swish).astype(BF)
     d2_ref[...] += nt(d_swish, wg_ref[...]) + nt(d_lift, wu_ref[...])
-    gg_ref[...] = tn(d_swish, x).astype(BF)
-    gu_ref[...] = tn(d_lift, x).astype(BF)
-    gd_ref[...] = tn(up, hidden).astype(BF)
+    xs = xs_ref[...]
+    gate = tn(d_swish, xs).astype(BF)
+    gk_ref[...] = gate[:, :half]
+    gs_ref[...] = gate[:, half:]
+    lifted = tn(d_lift, xs).astype(BF)
+    uk_ref[...] = lifted[:, :half]
+    us_out_ref[...] = lifted[:, half:]
+    down = tn(us_ref[...], hidden).astype(BF)
+    dk_ref[...] = down[:half]
+    ds_ref[...] = down[half:]
 
     @pl.when(tile == last)
     def _():
         res_ref[...] = total[...].astype(BF)
 
 
-def feed_forward(x, up, middle, wg, wu, wd):
+def feed_forward(x, up, middle, x_split, up_split, wg, wu, wd):
     rows, width = x.shape
     ff = wg.shape[1]
     tile = 256
+    half = width // 2
     whole = pl.BlockSpec((rows, width), lambda t: (0, 0))
     across = pl.BlockSpec((width, tile), lambda t: (0, t))
     down = pl.BlockSpec((tile, width), lambda t: (t, 0))
+    tall = pl.BlockSpec((tile, half), lambda t: (t, 0))
+    wide = pl.BlockSpec((half, tile), lambda t: (0, t))
+    tall_shape = jax.ShapeDtypeStruct((ff, half), BF)
+    wide_shape = jax.ShapeDtypeStruct((half, ff), BF)
     return pl.pallas_call(
         ff_kernel,
         grid=(ff // tile,),
-        in_specs=[whole, whole, whole, across, across, down],
-        out_specs=[whole, whole, down, down, across],
+        in_specs=[whole, whole, whole, whole, whole, across, across, down],
+        out_specs=[whole, whole, tall, tall, tall, tall, wide, wide],
         out_shape=[
             jax.ShapeDtypeStruct((rows, width), BF),
             jax.ShapeDtypeStruct((rows, width), F32),
-            jax.ShapeDtypeStruct((ff, width), BF),
-            jax.ShapeDtypeStruct((ff, width), BF),
-            jax.ShapeDtypeStruct((width, ff), BF),
+            *([tall_shape] * 4),
+            *([wide_shape] * 2),
         ],
         scratch_shapes=[pltpu.VMEM((rows, width), F32)],
         compiler_params=pltpu.CompilerParams(vmem_limit_bytes=VMEM_BYTES),
@@ -464,7 +517,115 @@
             flops=18 * rows * width * ff, bytes_accessed=12 * width * ff, transcendentals=rows * ff
         ),
         name="feed_forward",
-    )(x, up, middle, wg, wu, wd)
+    )(x, up, middle, x_split, up_split, wg, wu, wd)
+
+
+def input_kernel(
+    d_ref, w_ref, in_ref, mid_ref, gain_ref, out_ref, total,
+):
+    head = pl.program_id(0)
+
+    @pl.when(head == 0)
+    def _():
+        total[...] = jnp.zeros_like(total)
+
+    total[...] += nt(d_ref[0], w_ref[0])
+
+    @pl.when(head == pl.num_programs(0) - 1)
+    def _():
+        inputs = in_ref[...].astype(F32)
+        scale = lax.rsqrt(jnp.mean(inputs * inputs, -1, keepdims=True) + EPS)
+        grad = total[...]
+        scaled = grad * gain_ref[...]
+        mean = jnp.mean(scaled * inputs, -1, keepdims=True)
+        out_ref[...] = (
+            scale * scaled - inputs * (scale * scale * scale * mean) + mid_ref[...]
+        ).astype(BF)
+
+
+def input_gradient(d_pre, weights, tokens, grad_middle, gain):
+    heads, rows, columns = d_pre.shape
+    width = tokens.shape[1]
+    whole = lambda shape: pl.BlockSpec(shape, lambda h: (0,) * len(shape))
+    return pl.pallas_call(
+        input_kernel,
+        grid=(heads,),
+        in_specs=[
+            pl.BlockSpec((1, rows, columns), lambda h: (h, 0, 0)),
+            pl.BlockSpec((1, width, columns), lambda h: (h, 0, 0)),
+            whole((rows, width)),
+            whole((rows, width)),
+            whole((1, width)),
+        ],
+        out_specs=whole((rows, width)),
+        out_shape=jax.ShapeDtypeStruct((rows, width), BF),
+        scratch_shapes=[pltpu.VMEM((rows, width), F32)],
+        compiler_params=pltpu.CompilerParams(vmem_limit_bytes=VMEM_BYTES),
+        cost_estimate=pl.CostEstimate(
+            flops=2 * rows * heads * columns * width,
+            bytes_accessed=2 * heads * columns * (rows + width),
+            transcendentals=0,
+        ),
+        name="input_gradient",
+    )(d_pre, weights, tokens, grad_middle, gain)
+
+
+def owner_bits(skip):
+    sizes = {axis: lax.axis_size(axis) for axis in ("ctx", "fsdp")}
+    bits = [
+        (axis, 1 << i)
+        for axis in ("ctx", "fsdp")
+        for i in reversed(range(sizes[axis].bit_length() - 1))
+    ]
+    return bits[: len(bits) - skip]
+
+
+def swapped(value, axis, bit):
+    return lax.ppermute(value, axis, [(i, i ^ bit) for i in range(lax.axis_size(axis))])
+
+
+class Halving:
+    def __init__(self, value, bits, order):
+        self.left = list(bits)
+        self.order = order + [b for b in reversed(bits) if b not in order]
+        self.dtype = value.dtype
+        rows = value.shape[0] >> len(bits)
+        self.value = value.reshape(*([2] * len(bits)), rows, *value.shape[1:])
+
+    def start(self):
+        axis, bit = self.order[0]
+        dim = self.left.index(self.order[0])
+        mine = lax.axis_index(axis) // bit % 2
+        self.keep = lax.dynamic_index_in_dim(self.value, mine, dim, False)
+        self.send = lax.dynamic_index_in_dim(self.value, 1 - mine, dim, False)
+
+    def finish(self):
+        axis, bit = self.order.pop(0)
+        self.left.remove((axis, bit))
+        got = swapped(self.send, axis, bit)
+        self.value = (self.keep.astype(F32) + got.astype(F32)).astype(self.dtype)
+
+    def result(self):
+        while self.order:
+            self.start()
+            self.finish()
+        return self.value
+
+
+def around(value, axis, stride):
+    size = lax.axis_size(axis)
+    place = lax.axis_index(axis)
+    ring = [(i, (i + stride) % size) for i in range(size)]
+    across = [(i, i ^ 1) for i in range(size)]
+    every = jnp.zeros((size, *value.shape), value.dtype)
+    for hop in range(size // stride):
+        source = lax.rem(place - hop * stride + size, size)
+        every = lax.dynamic_update_index_in_dim(every, value, source, 0)
+        other = lax.ppermute(value, axis, across)
+        if hop + 1 < size // stride:
+            value = lax.ppermute(value, axis, ring)
+        every = lax.dynamic_update_index_in_dim(every, other, source ^ 1, 0)
+    return every
 
 
 def body(
@@ -496,7 +657,6 @@
     column = head * HEAD_SIZE
     slots = rows // C
     every = micros * rows
-    both = ("ctx", "fsdp")
 
     def gathered(w):
         return lax.all_gather(w, "fsdp", axis=0, tiled=True)
@@ -504,47 +664,88 @@
     def of_head(w, axis):
         return lax.dynamic_slice_in_dim(w, column, HEAD_SIZE, axis)
 
-    inputs = tokens.reshape(every, width).astype(F32)
-    first_scale = lax.rsqrt(jnp.mean(inputs * inputs, -1, keepdims=True) + EPS)
-    normed = (inputs * first_scale * norm_first).astype(BF)
-    x = lax.all_gather(normed.reshape(micros, rows, width), "ctx", axis=0)
-    mine = lax.rem(place, share) // copies * own
-    if share > 1:
-        x = lax.dynamic_slice_in_dim(x, mine, own, 1)
-    x = x.reshape(count, own, slots, C, width)
-    own_lengths = lax.dynamic_slice_in_dim(lengths[:, 0], mine, own, 0)
     projections = (w_query, w_key, w_value, w_mixgate)
     w_head = gathered(jnp.concatenate([of_head(w, 1) for w in projections], 1))
     taps = of_head(conv_weight, 2).transpose(1, 0, 2).reshape(taps_count, 3 * HEAD_SIZE)
     ridge = jnp.exp(of_head(ridge_log, 0))[None]
-    gated_head, pre, mixed, states = attention_forward(own_lengths, x, w_head, taps, ridge)
-
-    def to_rows(value):
-        columns = value.shape[-1]
-        value = lax.all_to_all(value.reshape(count, own, rows, columns), "ctx", 0, 0)
-        value = value.reshape(HEAD_COUNT, share // copies, copies, own, rows, columns)[:, :, 0]
-        value = value.reshape(HEAD_COUNT, micros, rows, columns)
-        return value.transpose(1, 2, 0, 3).reshape(every, HEAD_COUNT, columns)
-
-    def to_heads(value):
-        value = value.reshape(micros, rows, HEAD_COUNT, HEAD_SIZE).transpose(2, 0, 1, 3)
-        value = value.reshape(HEAD_COUNT, share // copies, 1, own, rows, HEAD_SIZE)
-        value = jnp.broadcast_to(value, (*value.shape[:2], copies, *value.shape[3:]))
-        value = lax.all_to_all(value.reshape(count, own, rows, HEAD_SIZE), "ctx", 0, 0)
-        return value.reshape(count, own, slots, C, HEAD_SIZE)
-
     full_output = gathered(w_output)
     full_ffgate = gathered(w_ffgate)
     full_ffup = gathered(w_ffup)
     full_ffdown = gathered(w_ffdown)
-    gated = to_rows(gated_head).reshape(every, width)
-    middle = inputs + nn(gated, full_output)
+    inputs = tokens.reshape(micros, rows, width).astype(F32)
+    first_scale = lax.rsqrt(jnp.mean(inputs * inputs, -1, keepdims=True) + EPS)
+    normed = (inputs * first_scale * norm_first).astype(BF)
+    mine = lax.rem(place, share) // copies * own
+    own_lengths = lax.dynamic_slice_in_dim(lengths[:, 0], mine, own, 0)
+
+    def to_rows(value):
+        columns = value.shape[-1]
+        value = value.reshape(count, -1, rows, columns)
+        value = lax.all_to_all(value, "ctx", 0, 0)
+        value = value.reshape(HEAD_COUNT, share // copies, copies, -1, columns)[:, :, 0]
+        return value.reshape(HEAD_COUNT, -1, columns)
+
+    def to_heads(value):
+        value = value.reshape(share // copies, -1, rows, HEAD_COUNT, HEAD_SIZE)
+        value = value.transpose(3, 0, 1, 2, 4)[:, :, None]
+        value = jnp.broadcast_to(value, (*value.shape[:2], copies, *value.shape[3:]))
+        value = value.reshape(count, -1, rows, HEAD_SIZE)
+        value = lax.all_to_all(value, "ctx", 0, 0)
+        return value.reshape(count, -1, slots, C, HEAD_SIZE)
+
+    lanes = micros if share == 1 else 1
+    states = []
+    middles = []
+    gateds = []
+    for lane in range(lanes):
+        part = normed[lane : lane + 1] if lanes > 1 else normed
+        x = around(part, "ctx", 2)
+        if share > 1:
+            x = lax.dynamic_slice_in_dim(x, mine, own, 1)
+        x = x.reshape(count, -1, slots, C, width)
+        lane_lengths = own_lengths[lane : lane + 1] if lanes > 1 else own_lengths
+        gated_head, pre, mixed, prefix = attention_forward(lane_lengths, x, w_head, taps, ridge)
+        states.append((lane_lengths, x, pre, mixed, prefix))
+        gated = to_rows(gated_head).transpose(1, 0, 2).reshape(-1, width)
+        before = inputs[lane] if lanes > 1 else inputs.reshape(every, width)
+        gateds.append(gated)
+        middles.append(before + nn(gated, full_output))
+    gated = jnp.concatenate(gateds, 0)
+    middle = jnp.concatenate(middles, 0)
     second_scale = lax.rsqrt(jnp.mean(middle * middle, -1, keepdims=True) + EPS)
     normed_two = (middle * second_scale * norm_second).astype(BF)
     upstream = out_grad.reshape(every, width)
-    result, grad_two, gate_t, up_t, down_t = feed_forward(
-        normed_two, upstream, middle, full_ffgate, full_ffup, full_ffdown
-    )
+    core = lax.axis_index("fsdp") % 2
+    devices = count * shards
+    half = width // 2
+
+    def halves(value):
+        return [lax.dynamic_slice_in_dim(value, c * half, half, 1) for c in (core, 1 - core)]
+
+    owned = upstream.reshape(every, devices // 2, 2, width // devices)
+    up_split = jnp.concatenate(
+        [
+            lax.dynamic_index_in_dim(owned, c, 2, False).reshape(every, half)
+            for c in (core, 1 - core)
+        ],
+        1,
+    )
+    x_split = jnp.concatenate(halves(normed_two), 1)
+    result, grad_two, gate_keep, gate_send, up_keep, up_send, down_keep, down_send = feed_forward(
+        normed_two, upstream, middle, x_split, up_split, full_ffgate, full_ffup, full_ffdown
+    )
+
+    def joined(keep, send, order):
+        got = swapped(send, "fsdp", 1)
+        value = (keep.astype(F32) + got.astype(F32)).astype(BF)
+        return Halving(value, owner_bits(1), order)
+
+    row, side = ("fsdp", 2), ("ctx", 1)
+    sums = [
+        joined(gate_keep, gate_send, [row, side]),
+        joined(up_keep, up_send, [side, row]),
+        joined(down_keep, down_send, [row, side]),
+    ]
     scaled_two = grad_two * norm_second
     gain_second = jnp.sum(grad_two * middle * second_scale, 0)
     grad_middle = (
@@ -553,59 +754,81 @@
         + upstream.astype(F32)
     )
     grad_branch = grad_middle.astype(BF)
-    output_t = tn(grad_branch, gated).astype(BF)
-    grad_gated = nt(grad_branch, full_output).astype(BF)
-    d_pre, dw, dtaps, dridge = attention_backward(
-        own_lengths, x, to_heads(grad_gated), pre, mixed, states, taps, ridge
-    )
-
-    def scattered(value):
-        return lax.psum_scatter(value, both, scatter_dimension=0, tiled=True).astype(F32).T
-
-    grad_ffgate = scattered(gate_t)
-    grad_ffup = scattered(up_t)
-    grad_ffdown = scattered(down_t)
-    grad_output = scattered(output_t)
-
+    gated_keep, gated_send = halves(gated)
+    sums.append(
+        joined(
+            tn(grad_branch, gated_keep).astype(BF), tn(grad_branch, gated_send).astype(BF), [side, row]
+        )
+    )
+    late = lax.optimization_barrier((gated, *projections))[1:]
+    late = jnp.stack([w.reshape(-1, HEAD_COUNT, HEAD_SIZE) for w in late], 2)
+    late = late.transpose(1, 0, 2, 3).reshape(HEAD_COUNT, -1, 4 * HEAD_SIZE)
+    full = lax.all_gather(late, "fsdp", axis=1, tiled=True)
+    span = every // lanes
+    pieces = []
+    d_rows = []
+    for lane in range(lanes):
+        at = slice(lane * span, (lane + 1) * span)
+        grad_gated = nt(grad_branch[at], full_output).astype(BF)
+        lane_lengths, x, pre, mixed, prefix = states[lane]
+        grad_heads = to_heads(grad_gated)
+        if lane == 0:
+            for part in sums:
+                part.start()
+            tied = lax.optimization_barrier((grad_heads, *[part.send for part in sums]))
+            grad_heads = tied[0]
+            for part, send in zip(sums, tied[1:]):
+                part.send = send
+                part.finish()
+        d_pre, dw, dtaps, dridge = attention_backward(
+            lane_lengths, x, grad_heads, pre, mixed, prefix, taps, ridge
+        )
+        pieces.append((dw, dtaps, dridge))
+        d_rows.append(to_rows(d_pre))
+    dw, dtaps, dridge = (sum(values) for values in zip(*pieces))
+    if copies > 1:
+        counts = lax.rem(place, copies) == 0
+        dw, dtaps, dridge = (jnp.where(counts, v, 0.0) for v in (dw, dtaps, dridge))
+    gain_first = jnp.sum(w_head.astype(F32).T * dw, 0) / norm_first
     piece = HEAD_SIZE // share // shards
     dw = dw.reshape(4, share, shards, piece, width).transpose(1, 2, 0, 3, 4).astype(BF)
-    small = jnp.concatenate(
-        [
-            dtaps[:taps_count].reshape(taps_count, 3, HEAD_SIZE).transpose(1, 0, 2).reshape(3 * taps_count, HEAD_SIZE),
-            dridge * ridge,
-        ],
-        0,
-    )
-    small = small.reshape(-1, share, shards, piece).transpose(1, 2, 0, 3)
     if share > 1:
         groups = [[h * share + i for i in range(share)] for h in range(HEAD_COUNT)]
-        counts = lax.rem(place, copies) == 0
-        dw = jnp.where(counts, dw, jnp.zeros_like(dw))
-        small = jnp.where(counts, small, 0.0)
         dw = lax.psum_scatter(dw, "ctx", scatter_dimension=0, axis_index_groups=groups)
-        small = lax.psum_scatter(small, "ctx", scatter_dimension=0, axis_index_groups=groups)
     else:
         dw = dw[0]
-        small = small[0]
     dw = lax.psum_scatter(dw, "fsdp", scatter_dimension=0).astype(F32).transpose(0, 2, 1)
-    small = lax.psum_scatter(small, "fsdp", scatter_dimension=0)
-
-    full = jnp.stack([gathered(w) for w in projections], 1)
-    full = full.reshape(width, 4, HEAD_COUNT, HEAD_SIZE).transpose(0, 2, 1, 3).reshape(width, -1)
-    grad_normed = nt(to_rows(d_pre).reshape(every, -1), full)
-    scaled_first = grad_normed * norm_first
-    gain_first = jnp.sum(grad_normed * inputs * first_scale, 0)
-    grad_inputs = (
-        first_scale * scaled_first
-        - inputs * first_scale**3 * jnp.mean(scaled_first * inputs, -1, keepdims=True)
-        + grad_middle
-    )
-    gains = jnp.stack([gain_first, gain_second], 0)
-    gains = lax.psum_scatter(gains, both, scatter_dimension=1, tiled=True)
+    dtaps = dtaps[:taps_count].reshape(taps_count, 3, HEAD_SIZE).transpose(1, 0, 2)
+    small = jnp.concatenate([dtaps.reshape(3 * taps_count, HEAD_SIZE), dridge * ridge], 0)
+    small = lax.dynamic_update_slice_in_dim(
+        jnp.zeros((small.shape[0], width), F32), small, column, 1
+    )
+    small = jnp.concatenate([small, gain_first[None], gain_second[None]], 0)
+    small = small.reshape(-1, devices, width // devices).transpose(1, 0, 2)
+    small = Halving(small, owner_bits(0), []).result()[0]
+
+    def columns_of(part):
+        rows_now = part.result()
+        rows_now = rows_now.reshape(2, -1, half)
+        keep = lax.dynamic_index_in_dim(rows_now, core, 0, False)
+        got = swapped(lax.dynamic_index_in_dim(rows_now, 1 - core, 0, False), "fsdp", 1)
+        pair = jnp.where(core == 0, jnp.stack([keep, got]), jnp.stack([got, keep]))
+        return pair.astype(F32).transpose(0, 2, 1).reshape(width, -1)
+
+    grad_ffgate, grad_ffup, grad_output = (columns_of(sums[i]) for i in (0, 1, 3))
+    grad_ffdown = sums[2].result().astype(F32).T
+
+    out_rows = []
+    for lane in range(lanes):
+        at = slice(lane * span, (lane + 1) * span)
+        grad_inputs = input_gradient(
+            d_rows[lane], full, tokens.reshape(every, width)[at], grad_middle[at], norm_first[None]
+        )
+        out_rows.append(grad_inputs)
     conv_shard = small[: 3 * taps_count].reshape(3, taps_count, -1)
     return (
         result.reshape(tokens.shape),
-        grad_inputs.astype(BF).reshape(tokens.shape),
+        jnp.concatenate(out_rows, 0).reshape(tokens.shape),
         dw[0],
         dw[1],
         dw[2],
@@ -615,8 +838,8 @@
         grad_ffup,
         grad_ffdown,
         conv_shard,
-        gains[0],
-        gains[1],
+        small[3 * taps_count + 1],
+        small[3 * taps_count + 2],
         small[3 * taps_count],
     )
 

time: 1210 us -> 576 us (0.48)
  waiting for transfers between devices: 935 us -> 190 us
  starting transfers between devices: 15 us -> 80.9 us
  local copies, waits for them, and re-layouts: 41.2 us -> 78.9 us
  other arithmetic: 29 us -> 46.5 us
    reduce_scatter x4 -> x0, waiting for transfers between devices: 463 us -> none  [scattered(): lax.psum_scatter(value, both, scatter_dimension=0, tiled=True).astype(F32)]
    ppermute x0 -> x42, waiting for transfers between devices: none -> 166 us  [the longest x28 124 us: swapped(): lax.ppermute(value, axis, [(i, i ^ bit) for i in range(lax.axis_size(axis...]
    unnamed x17 -> x7, waiting for transfers between devices: 136 us -> 2.48 us
    all_gather x1, waiting for transfers between devices: 128 us -> 0.02 us  [body(): full = lax.all_gather(late, 'fsdp', axis=1, tiled=True)]
    all_to_all x3 -> x6, waiting for transfers between devices: 116 us -> 8.35 us  [the longest x2 8.34 us: to_heads(): value = lax.all_to_all(value, 'ctx', 0, 0)]
    all_gather x9 -> x5, waiting for transfers between devices: 92.4 us -> 12.6 us  [gathered(): return lax.all_gather(w, 'fsdp', axis=0, tiled=True)]
    ppermute x0 -> x42, starting transfers between devices: none -> 40 us  [the longest x28 28.4 us: swapped(): lax.ppermute(value, axis, [(i, i ^ bit) for i in range(lax.axis_size(axis...]
    all_to_all x3 -> x6, starting transfers between devices: 13.7 us -> 40.7 us  [the longest x4 23.7 us: to_rows(): value = lax.all_to_all(value, 'ctx', 0, 0)]
  transfers between devices with their start and end apart: 19 -> 55, of which waited for: 12 -> 20; matrix products, arithmetic and copies ran while one was open for 6% -> 22% of each run, Pallas kernels for 12% -> 23%
where the time goes in v2:
time: 576 us; the launch traced here: 566 us
  waiting for transfers between devices  190 us (33%)
  Pallas kernels  141 us (24%)
  starting transfers between devices  80.9 us (14%)
  local copies, waits for them, and re-layouts  78.9 us (14%)
  other arithmetic  46.5 us (8%)
  between operations  15.5 us (3%)
  matrix products  13.3 us (2%)
    ppermute x28, waiting for transfers between devices, swapped(): lax.ppermute(value, axis, [(i, i ^ bit) for i in range(lax.axis_size(axis...  124 us
    pallas_call x2, Pallas kernels, attention_backward(): pl.pallas_call(partial(backward_kernel, count, steps), grid=(micros, step...  49.1 us
    pallas_call x1, Pallas kernels, feed_forward(): pl.pallas_call(ff_kernel, grid=(ff // tile,), in_specs=[whole, whole, who...  41.8 us
    ppermute x6, waiting for transfers between devices, around(): value = lax.ppermute(value, axis, ring)  38.1 us
    pallas_call x2, Pallas kernels, attention_forward(): pl.pallas_call(partial(forward_kernel, count), grid=(micros, steps), in_s...  30.5 us
    ppermute x28, starting transfers between devices, swapped(): lax.ppermute(value, axis, [(i, i ^ bit) for i in range(lax.axis_size(axis...  28.4 us
    all_to_all x4, starting transfers between devices, to_rows(): value = lax.all_to_all(value, 'ctx', 0, 0)  23.7 us
    pallas_call x2, Pallas kernels, input_gradient(): pl.pallas_call(input_kernel, grid=(heads,), in_specs=[pl.BlockSpec((1, ro...  19.5 us
  transfers between devices with their start and end apart: 55, of which 20 were waited for; matrix products, arithmetic and copies ran while one was open for 22% of the time, Pallas kernels for 23%

profile of v2, /device:TPU:0, one launch (start us, length us, event | category | flops | bytes accessed | tf_op | source)
XLA Modules:
  0.0 565.8 jit_solution(4690672718920338829)
XLA Ops:
  38.9 6.8 %collective-permute-done.8 = bf16[1,256,1024]{2,1,0:T(8,128)(2,1)} collective-permute-done((bf16[1,256,1024]{2,1,0:T(8,128)(2,1)}, bf16[1,256,1024]{2,1,0:T(8,128)(2,1)}, u32[]{:S(2)}, u32[]{:S(2)}) %collective-permute-start.8) | collective-permute-done | bytes 524320 | tf_op jit(solution)/shard_map/ppermute | solution.py:626
  57.2 10.9 %collective-permute-done.10 = bf16[1,256,1024]{2,1,0:T(8,128)(2,1)S(1)} collective-permute-done((bf16[1,256,1024]{2,1,0:T(8,128)(2,1)}, bf16[1,256,1024]{2,1,0:T(8,128)(2,1)S(1)}, u32[]{:S(2)}, u32[]{:S(2)}) %collective-permute-start.10) | collective-permute-done | bytes 524320 | tf_op jit(solution)/shard_map/ppermute | solution.py:626
  70.9 8.4 %collective-permute-done.5 = bf16[1,256,1024]{2,1,0:T(8,128)(2,1)S(1)} collective-permute-done((bf16[1,256,1024]{2,1,0:T(8,128)(2,1)S(1)}, bf16[1,256,1024]{2,1,0:T(8,128)(2,1)S(1)}, u32[]{:S(2)}, u32[]{:S(2)}) %collective-permute-start.5) | collective-permute-done | bytes 524320 | tf_op jit(solution)/shard_map/ppermute | solution.py:626
  80.4 8.7 %collective-permute-done.12 = bf16[1,256,1024]{2,1,0:T(8,128)(2,1)S(1)} collective-permute-done((bf16[1,256,1024]{2,1,0:T(8,128)(2,1)S(1)}, bf16[1,256,1024]{2,1,0:T(8,128)(2,1)S(1)}, u32[]{:S(2)}, u32[]{:S(2)}) %collective-permute-start.12) | collective-permute-done | bytes 524320 | tf_op jit(solution)/shard_map/ppermute | solution.py:626
  99.9 15.3 %attn_forward.2 = (bf16[8,1,2,128,128]{4,3,2,1,0:T(8,128)(2,1)}, f32[8,1,2,128,512]{4,3,2,1,0:T(8,128)}, f32[8,1,2,128,128]{4,3,2,1,0:T(8,128)}, f32[8,1,2,2,128,128]{5,4,3,2,1,0:T(8,128)}) custom-call(s32[1]{0:T(128)} %bitcast.1.len_ref, bf16[8,1,2,128,1024]{4,3,2,1,0:T(8,128)(2,1)} %bitcast.320, bf16[1024,512]{1,0:T(8,128)(2,1)} %copy.170.w_ref, ...), custom_call_target="tpu_custom_call" | custom-call | flops 2885681152 | bytes 12582912 | tf_op jit(solution)/shard_map/attn_forward/pallas_call | solution.py:193
  117.2 6.6 %all-to-all-start = ((bf16[8,1,256,128]{2,3,1,0:T(8,128)(2,1)}), bf16[8,1,256,128]{2,3,1,0:T(8,128)(2,1)S(1)}, u32[]{:S(2)}, u32[]{:S(2)}) async-start(bf16[8,1,256,128]{2,3,1,0:T(8,128)(2,1)} %copy.171), calls=%async_computation | async-start | bytes 1048576 | tf_op jit(solution)/shard_map/all_to_all | solution.py:684
  127.5 15.2 %attn_forward.3 = (bf16[8,1,2,128,128]{4,3,2,1,0:T(8,128)(2,1)}, f32[8,1,2,128,512]{4,3,2,1,0:T(8,128)}, f32[8,1,2,128,128]{4,3,2,1,0:T(8,128)}, f32[8,1,2,2,128,128]{5,4,3,2,1,0:T(8,128)}) custom-call(s32[1]{0:T(128)} %bitcast.20.len_ref, bf16[8,1,2,128,1024]{4,3,2,1,0:T(8,128)(2,1)} %bitcast.31.x_ref, bf16[1024,512]{1,0:T(8,128)(2,1)} %copy.170.w_ref, ...), custom_call_target="tpu_custom_call" | custom-call | flops 2885681152 | bytes 12582912 | tf_op jit(solution)/shard_map/attn_forward/pallas_call | solution.py:193
  150.7 6.6 %maximum_bitcast_fusion = bf16[8,256,4,128]{3,2,1,0:T(4,128)(2,1)S(1)} fusion(bf16[256,8,1,128]{3,2,0,1:T(2,128)(2,1)} %copy.185, bf16[256,8,1,128]{3,2,0,1:T(2,128)(2,1)} %copy.184, bf16[256,8,1,128]{3,2,0,1:T(2,128)(2,1)} %copy.183, bf16[256,8,1,128]{3,2,0,1:T(2,128)(2,1)} %copy.182), kind=kLoop, calls=%fused_computation.10 | loop fusion | flops 8388608 | bytes 4194304 | tf_op jit(solution)/shard_map/transpose | solution.py:765
  176.3 12.6 %all-gather.15.cloned.1.call-done.wd_ref = bf16[2816,1024]{1,0:T(8,128)(2,1)} async-done(((bf16[704,1024]{1,0:T(8,128)(2,1)}), bf16[2816,1024]{1,0:T(8,128)(2,1)}) %all-gather.15.cloned.1.call-update) | async-done | bytes 5767184 | tf_op jit(solution)/shard_map/all_gather | solution.py:662
  188.9 41.8 %feed_forward.1 = (bf16[512,1024]{1,0:T(8,128)(2,1)}, f32[512,1024]{1,0:T(8,128)}, bf16[2816,512]{1,0:T(8,128)(2,1)}, bf16[2816,512]{1,0:T(8,128)(2,1)}, bf16[28...) custom-call(bf16[512,1024]{1,0:T(8,128)(2,1)} %copy-done.22, ...), custom_call_target="tpu_custom_call" | custom-call | flops 26575110144 | bytes 34603008 | tf_op jit(solution)/shard_map/feed_forward/pallas_call | solution.py:503
  237.6 13.4 %all-to-all-start.4 = ((bf16[8,1,256,128]{3,2,1,0:T(8,128)(2,1)}), bf16[8,1,256,128]{3,2,1,0:T(8,128)(2,1)}, u32[]{:S(2)}, u32[]{:S(2)}) async-start(bf16[8,1,256,128]{3,2,1,0:T(8,128)(2,1)} %bitcast.316), calls=%async_computation.4 | async-start | bytes 1048576 | tf_op jit(solution)/shard_map/all_to_all | solution.py:693
  257.5 8.3 %all-to-all-done.4 = bf16[8,1,256,128]{3,2,1,0:T(8,128)(2,1)} async-done(((bf16[8,1,256,128]{3,2,1,0:T(8,128)(2,1)}), bf16[8,1,256,128]{3,2,1,0:T(8,128)(2,1)}, u32[]{:S(2)}, u32[]{:S(2)}) %all-to-all-start.4) | async-done | bytes 524320 | tf_op jit(solution)/shard_map/all_to_all | solution.py:693
  269.5 24.5 %attn_backward.3 = (bf16[8,1,2,128,512]{4,3,2,1,0:T(8,128)(2,1)}, f32[512,1024]{1,0:T(8,128)}, f32[8,384]{1,0:T(8,128)}, f32[1,128]{1,0:T(1,128)}) custom-call(s32[1]{0:T(128)} %bitcast.20.len_ref, bf16[8,1,2,128,1024]{4,3,2,1,0:T(8,128)(2,1)} %bitcast.31.x_ref, bf16[8,1,2,128,128]{4,3,2,1,0:T(8,128)(2,1)} %bitcast.65.g_ref, ...), custom_call_target="tpu_custom_call" | custom-call | flops 3758096384 | bytes 12582912 | tf_op jit(solution)/shard_map/attn_backward/pallas_call | solution.py:402
  315.8 24.7 %attn_backward.2 = (bf16[8,1,2,128,512]{4,3,2,1,0:T(8,128)(2,1)}, f32[512,1024]{1,0:T(8,128)}, f32[8,384]{1,0:T(8,128)}, f32[1,128]{1,0:T(1,128)}) custom-call(s32[1]{0:T(128)} %bitcast.1.len_ref, bf16[8,1,2,128,1024]{4,3,2,1,0:T(8,128)(2,1)} %bitcast.321, bf16[8,1,2,128,128]{4,3,2,1,0:T(8,128)(2,1)} %bitcast.334, ...), custom_call_target="tpu_custom_call" | custom-call | flops 3758096384 | bytes 12582912 | tf_op jit(solution)/shard_map/attn_backward/pallas_call | solution.py:402
  362.5 11.3 %collective-permute-done.18 = bf16[2,2,2,64,512]{4,3,2,1,0:T(8,128)(2,1)} collective-permute-done((bf16[2,2,2,64,512]{4,3,2,1,0:T(8,128)(2,1)}, bf16[2,2,2,64,512]{4,3,2,1,0:T(8,128)(2,1)}, u32[]{:S(2)}, u32[]{:S(2)}) %collective-permute-start.18) | collective-permute-done | bytes 524320 | tf_op jit(solution)/shard_map/ppermute | solution.py:584
  375.3 41.6 %collective-permute-done.39 = f32[2,2,1,15,32]{4,1,3,0,2:T(2,128)S(1)} collective-permute-done((f32[2,2,1,15,32]{4,1,3,0,2:T(2,128)S(1)}, f32[2,2,1,15,32]{4,1,3,0,2:T(2,128)S(1)}, u32[]{:S(2)}, u32[]{:S(2)}) %collective-permute-start.39) | collective-permute-done | bytes 7712 | tf_op jit(solution)/shard_map/ppermute | solution.py:584
  418.7 13.9 %collective-permute-done.19 = bf16[2,2,64,512]{3,2,1,0:T(8,128)(2,1)S(1)} collective-permute-done((bf16[2,2,64,512]{3,2,1,0:T(8,128)(2,1)S(1)}, bf16[2,2,64,512]{3,2,1,0:T(8,128)(2,1)S(1)}, u32[]{:S(2)}, u32[]{:S(2)}) %collective-permute-start.19) | collective-permute-done | bytes 262176 | tf_op jit(solution)/shard_map/ppermute | solution.py:584
  466.4 9.7 %input_gradient.3 = bf16[256,1024]{1,0:T(8,128)(2,1)} custom-call(bf16[8,256,512]{2,1,0:T(8,128)(2,1)} %bitcast.327, bf16[8,1024,512]{2,1,0:T(8,128)(2,1)} %all-gather.17.cloned.1.call-done.w_ref, bf16[256,1024]{1,0:T(8,128)(2,1)} %get-tuple-element.177.in_ref, f32[256,1024]{1,0:T(8,128)} %get-tuple-element.173.mid_ref, f32[1,1024]{1,0:T(1,128)} %bitcast.365), custom_call_target="tpu_custom_call" | custom-call | flops 2147483648 | bytes 10485760 | tf_op jit(solution)/shard_map/input_gradient/pallas_call | solution.py:550
  483.0 16.7 %collective-permute-done.24 = bf16[2,2,176,512]{3,2,1,0:T(8,128)(2,1)} collective-permute-done((bf16[2,2,176,512]{3,2,1,0:T(8,128)(2,1)}, bf16[2,2,176,512]{3,2,1,0:T(8,128)(2,1)}, u32[]{:S(2)}, u32[]{:S(2)}) %collective-permute-start.24) | collective-permute-done | bytes 720928 | tf_op jit(solution)/shard_map/ppermute | solution.py:584
  502.5 7.5 %collective-permute-done.35 = bf16[2,32,2816]{2,1,0:T(8,128)(2,1)S(1)} collective-permute-done((bf16[2,32,2816]{2,1,0:T(8,128)(2,1)S(1)}, bf16[2,32,2816]{2,1,0:T(8,128)(2,1)S(1)}, u32[]{:S(2)}, u32[]{:S(2)}) %collective-permute-start.35) | collective-permute-done | bytes 360480 | tf_op jit(solution)/shard_map/ppermute | solution.py:584
  514.3 8.9 %collective-permute-done.30 = bf16[2,176,512]{2,1,0:T(8,128)(2,1)S(1)} collective-permute-done((bf16[2,176,512]{2,1,0:T(8,128)(2,1)S(1)}, bf16[2,176,512]{2,1,0:T(8,128)(2,1)S(1)}, u32[]{:S(2)}, u32[]{:S(2)}) %collective-permute-start.30) | collective-permute-done | bytes 360480 | tf_op jit(solution)/shard_map/ppermute | solution.py:584
  523.4 8.4 %collective-permute-done.25 = bf16[2,176,512]{2,1,0:T(8,128)(2,1)S(1)} collective-permute-done((bf16[2,176,512]{2,1,0:T(8,128)(2,1)S(1)}, bf16[2,176,512]{2,1,0:T(8,128)(2,1)S(1)}, u32[]{:S(2)}, u32[]{:S(2)}) %collective-permute-start.25) | collective-permute-done | bytes 360480 | tf_op jit(solution)/shard_map/ppermute | solution.py:584
  532.1 9.4 %collective-permute-done.31 = bf16[176,512]{1,0:T(8,128)(2,1)S(1)} collective-permute-done((bf16[176,512]{1,0:T(8,128)(2,1)S(1)}, bf16[176,512]{1,0:T(8,128)(2,1)S(1)}, u32[]{:S(2)}, u32[]{:S(2)}) %collective-permute-start.31) | collective-permute-done | bytes 180256 | tf_op jit(solution)/shard_map/ppermute | solution.py:584
  546.7 9.8 %input_gradient.2 = bf16[256,1024]{1,0:T(8,128)(2,1)} custom-call(bf16[8,256,512]{2,1,0:T(8,128)(2,1)} %bitcast.59.d_ref, bf16[8,1024,512]{2,1,0:T(8,128)(2,1)} %all-gather.17.cloned.1.call-done.w_ref, bf16[256,1024]{1,0:T(8,128)(2,1)} %get-tuple-element.176.in_ref, f32[256,1024]{1,0:T(8,128)} %get-tuple-element.172.mid_ref, f32[1,1024]{1,0:T(1,128)} %bitcast.366), custom_call_target="tpu_custom_call" | custom-call | flops 2147483648 | bytes 10485760 | tf_op jit(solution)/shard_map/input_gradient/pallas_call | solution.py:550
  (336 shorter events, 209.3 us)
Async XLA Ops:
  7.2 84.2 %all-gather.7.cloned.1.call-start = ((), (), s32[]{:S(2)}) async-start(), calls=%async_computation.7 | async-start | bytes 1310720 | tf_op jit(solution)/shard_map/all_gather | solution.py:662
  10.2 156.2 %all-gather.9.cloned.1.call-start = ((), (), s32[]{:S(2)}) async-start(), calls=%async_computation.8 | async-start | bytes 2621440 | tf_op jit(solution)/shard_map/all_gather | solution.py:662
  11.0 165.3 %all-gather.11.cloned.1.call-start = ((), (), s32[]{:S(2)}) async-start(), calls=%async_computation.9 | async-start | bytes 7208960 | tf_op jit(solution)/shard_map/all_gather | solution.py:662
  11.7 164.5 %all-gather.13.cloned.1.call-start = ((), (), s32[]{:S(2)}) async-start(), calls=%async_computation.10 | async-start | bytes 7208960 | tf_op jit(solution)/shard_map/all_gather | solution.py:662
  12.3 176.5 %all-gather.15.cloned.1.call-start = ((), (), s32[]{:S(2)}) async-start(), calls=%async_computation.11 | async-start | bytes 7208960 | tf_op jit(solution)/shard_map/all_gather | solution.py:662
  68.1 55.8 %collective-permute-start.11 = (bf16[1,256,1024]{2,1,0:T(8,128)(2,1)S(1)}, bf16[1,256,1024]{2,1,0:T(8,128)(2,1)S(1)}, u32[]{:S(2)}, u32[]{:S(2)}) collective-permute-start(bf16[1,256,1024]{2,1,0:T(8,128)(2,1)S(1)} %collective-permute-done.10), channel_id=1, source_target_pairs={{0,4},{4,0},{8,12},{12,8},{16,20},{20,16},{24,28},{28,24},{1,5},{5... | collective-permute-start | bytes 1572872 | tf_op jit(solution)/shard_map/ppermute | solution.py:624
  89.2 36.4 %collective-permute-start.13 = (bf16[1,256,1024]{2,1,0:T(8,128)(2,1)S(1)}, bf16[1,256,1024]{2,1,0:T(8,128)(2,1)}, u32[]{:S(2)}, u32[]{:S(2)}) collective-permute-start(bf16[1,256,1024]{2,1,0:T(8,128)(2,1)S(1)} %collective-permute-done.12), channel_id=1, source_target_pairs={{0,4},{4,0},{8,12},{12,8},{16,20},{20,16},{24,28},{28,24},{1,5},{5... | collective-permute-start | bytes 1572872 | tf_op jit(solution)/shard_map/ppermute | solution.py:624
  150.7 315.7 %all-gather.17.cloned.1.call-start = ((), (), s32[]{:S(2)}) async-start(), calls=%async_computation.12 | async-start | bytes 10485760 | tf_op jit(solution)/shard_map/all_gather | solution.py:766
  230.6 66.6 %collective-permute-start.16 = (bf16[512,2816]{1,0:T(8,128)(2,1)}, bf16[512,2816]{1,0:T(8,128)(2,1)}, u32[]{:S(2)}, u32[]{:S(2)}) collective-permute-start(bf16[512,2816]{1,0:T(8,128)(2,1)} %get-tuple-element.56), channel_id=1, source_target_pairs={{0,1},{1,0},{2,3},{3,2},{4,5},{5,4},{6,7},{7,6},{8,9},{9,8},{10,11... | collective-permute-start | bytes 8650760 | tf_op jit(solution)/shard_map/ppermute | solution.py:584
  231.0 71.4 %collective-permute-start.15 = (bf16[2816,512]{1,0:T(8,128)(2,1)}, bf16[2816,512]{1,0:T(8,128)(2,1)}, u32[]{:S(2)}, u32[]{:S(2)}) collective-permute-start(bf16[2816,512]{1,0:T(8,128)(2,1)} %get-tuple-element.54), channel_id=1, source_target_pairs={{0,1},{1,0},{2,3},{3,2},{4,5},{5,4},{6,7},{7,6},{8,9},{9,8},{10,11... | collective-permute-start | bytes 8650760 | tf_op jit(solution)/shard_map/ppermute | solution.py:584
  254.2 39.8 %collective-permute-start.17 = (bf16[1024,512]{1,0:T(8,128)(2,1)}, bf16[1024,512]{1,0:T(8,128)(2,1)}, u32[]{:S(2)}, u32[]{:S(2)}) collective-permute-start(bf16[1024,512]{1,0:T(8,128)(2,1)} %convolution_convert_fusion), channel_id=1, source_target_pairs={{0,1},{1,0},{2,3},{3,2},{4,5},{5,4},{6,7},{7,6},{8,9},{9,8},{10,11... | collective-permute-start | bytes 3145736 | tf_op jit(solution)/shard_map/ppermute | solution.py:584
  254.2 53.3 %collective-permute-start.14 = (bf16[2816,512]{1,0:T(8,128)(2,1)}, bf16[2816,512]{1,0:T(8,128)(2,1)}, u32[]{:S(2)}, u32[]{:S(2)}) collective-permute-start(bf16[2816,512]{1,0:T(8,128)(2,1)} %get-tuple-element.52), channel_id=1, source_target_pairs={{0,1},{1,0},{2,3},{3,2},{4,5},{5,4},{6,7},{7,6},{8,9},{9,8},{10,11... | collective-permute-start | bytes 8650760 | tf_op jit(solution)/shard_map/ppermute | solution.py:584
  265.9 49.1 %all-to-all-start.2 = ((bf16[8,1,256,128]{3,2,1,0:T(8,128)(2,1)}), bf16[8,1,256,128]{3,2,1,0:T(8,128)(2,1)S(1)}, u32[]{:S(2)}, u32[]{:S(2)}) async-start(bf16[8,1,256,128]{3,2,1,0:T(8,128)(2,1)} %bitcast.317), calls=%async_computation.2 | async-start | bytes 1048576 | tf_op jit(solution)/shard_map/all_to_all | solution.py:693
  352.3 106.3 %all-to-all-start.5 = ((bf16[8,1,256,512]{3,2,1,0:T(8,128)(2,1)}), bf16[8,1,256,512]{3,2,1,0:T(8,128)(2,1)S(1)}, u32[]{:S(2)}, u32[]{:S(2)}) async-start(bf16[8,1,256,512]{3,2,1,0:T(8,128)(2,1)} %bitcast.340), calls=%async_computation.5 | async-start | bytes 4194304 | tf_op jit(solution)/shard_map/all_to_all | solution.py:684
  357.0 119.1 %reduce-scatter.2.cloned.1.call-start = ((), (), s32[]{:S(2)}) async-start(), calls=%async_computation.13 | async-start | bytes 1310720 | tf_op jit(solution)/shard_map/reduce_scatter | solution.py:800
  357.0 88.0 %collective-permute-start.33 = (bf16[2,2,2,32,2816]{4,3,0,1,2:T(8,128)(2,1)}, bf16[2,2,2,32,2816]{4,3,0,1,2:T(8,128)(2,1)}, u32[]{:S(2)}, u32[]{:S(2)}) collective-permute-start(bf16[2,2,2,32,2816]{4,3,0,1,2:T(8,128)(2,1)} %bitcast.345), channel_id=1, source_target_pairs={{0,2},{1,3},{2,0},{3,1},{4,6},{5,7},{6,4},{7,5},{8,10},{9,11},{10,... | collective-permute-start | bytes 4325384 | tf_op jit(solution)/shard_map/ppermute | solution.py:584
  358.6 92.0 %collective-permute-start.28 = (bf16[2,2,2,176,512]{4,3,2,1,0:T(8,128)(2,1)}, bf16[2,2,2,176,512]{4,3,2,1,0:T(8,128)(2,1)}, u32[]{:S(2)}, u32[]{:S(2)}) collective-permute-start(bf16[2,2,2,176,512]{4,3,2,1,0:T(8,128)(2,1)} %dynamic-slice_bitcast_fusion), channel_id=1, source_target_pairs={{0,4},{4,0},{8,12},{12,8},{16,20},{20,16},{24,28},{28,24},{1,5},{5... | collective-permute-start | bytes 4325384 | tf_op jit(solution)/shard_map/ppermute | solution.py:584
  360.5 94.4 %collective-permute-start.23 = (bf16[2,2,2,176,512]{4,3,2,1,0:T(8,128)(2,1)}, bf16[2,2,2,176,512]{4,3,2,1,0:T(8,128)(2,1)}, u32[]{:S(2)}, u32[]{:S(2)}) collective-permute-start(bf16[2,2,2,176,512]{4,3,2,1,0:T(8,128)(2,1)} %dynamic-slice_bitcast_fusion.1), channel_id=1, source_target_pairs={{0,2},{1,3},{2,0},{3,1},{4,6},{5,7},{6,4},{7,5},{8,10},{9,11},{10,... | collective-permute-start | bytes 4325384 | tf_op jit(solution)/shard_map/ppermute | solution.py:584
  362.3 54.6 %collective-permute-start.39 = (f32[2,2,1,15,32]{4,1,3,0,2:T(2,128)S(1)}, f32[2,2,1,15,32]{4,1,3,0,2:T(2,128)S(1)}, u32[]{:S(2)}, u32[]{:S(2)}) collective-permute-start(f32[2,2,1,15,32]{4,1,3,0,2:T(2,128)S(1)} %dynamic-slice_bitcast_fusion.18), channel_id=1, source_target_pairs={{0,4},{4,0},{8,12},{12,8},{16,20},{20,16},{24,28},{28,24},{1,5},{5... | collective-permute-start | bytes 23048 | tf_op jit(solution)/shard_map/ppermute | solution.py:584
  375.2 57.4 %collective-permute-start.19 = (bf16[2,2,64,512]{3,2,1,0:T(8,128)(2,1)S(1)}, bf16[2,2,64,512]{3,2,1,0:T(8,128)(2,1)S(1)}, u32[]{:S(2)}, u32[]{:S(2)}) collective-permute-start(bf16[2,2,64,512]{3,2,1,0:T(8,128)(2,1)S(1)} %dynamic-slice_bitcast_fusion.9), channel_id=1, source_target_pairs={{0,2},{1,3},{2,0},{3,1},{4,6},{5,7},{6,4},{7,5},{8,10},{9,11},{10,... | collective-permute-start | bytes 786440 | tf_op jit(solution)/shard_map/ppermute | solution.py:584
  458.1 41.7 %collective-permute-start.24 = (bf16[2,2,176,512]{3,2,1,0:T(8,128)(2,1)}, bf16[2,2,176,512]{3,2,1,0:T(8,128)(2,1)}, u32[]{:S(2)}, u32[]{:S(2)}) collective-permute-start(bf16[2,2,176,512]{3,2,1,0:T(8,128)(2,1)} %dynamic-slice_bitcast_fusion.4), channel_id=1, source_target_pairs={{0,4},{4,0},{8,12},{12,8},{16,20},{20,16},{24,28},{28,24},{1,5},{5... | collective-permute-start | bytes 2162696 | tf_op jit(solution)/shard_map/ppermute | solution.py:584
  460.0 86.7 %all-to-all-start.3 = ((bf16[8,1,256,512]{3,2,1,0:T(8,128)(2,1)}), bf16[8,1,256,512]{3,2,1,0:T(8,128)(2,1)}, u32[]{:S(2)}, u32[]{:S(2)}) async-start(bf16[8,1,256,512]{3,2,1,0:T(8,128)(2,1)} %bitcast.339), calls=%async_computation.3 | async-start | bytes 4194304 | tf_op jit(solution)/shard_map/all_to_all | solution.py:684
  482.9 40.3 %collective-permute-start.30 = (bf16[2,176,512]{2,1,0:T(8,128)(2,1)S(1)}, bf16[2,176,512]{2,1,0:T(8,128)(2,1)S(1)}, u32[]{:S(2)}, u32[]{:S(2)}) collective-permute-start(bf16[2,176,512]{2,1,0:T(8,128)(2,1)S(1)} %dynamic-slice_bitcast_fusion.7), channel_id=1, source_target_pairs={{0,8},{4,12},{8,0},{12,4},{16,24},{20,28},{24,16},{28,20},{1,9},{5... | collective-permute-start | bytes 1081352 | tf_op jit(solution)/shard_map/ppermute | solution.py:584
  510.1 34.2 %collective-permute-start.36 = (bf16[32,2816]{1,0:T(8,128)(2,1)S(1)}, bf16[32,2816]{1,0:T(8,128)(2,1)S(1)}, u32[]{:S(2)}, u32[]{:S(2)}) collective-permute-start(bf16[32,2816]{1,0:T(8,128)(2,1)S(1)} %dynamic-slice_bitcast_fusion.10), channel_id=1, source_target_pairs={{0,16},{4,20},{8,24},{12,28},{16,0},{20,4},{24,8},{28,12},{1,17},{... | collective-permute-start | bytes 540680 | tf_op jit(solution)/shard_map/ppermute | solution.py:584
  (76 other events, 979.3 us)
Sparse Core Ops, SparseCore 0:
  10.4 19.5 all-gather.6
  31.5 22.5 all-gather.8
  55.7 43.3 all-gather.10
  100.5 43.3 all-gather.12
  145.4 43.4 all-gather.14
  190.3 58.2 all-gather.16
  362.3 30.5 reduce-scatter.1
